TPU v7x, 512 devices: a whole 4x4x16 slice. The times are simulated.
512 devices in a mesh: seq: 32 (over x_hi, z), head: 4 (over y), dp: 4 (over x_lo, core).
Axes of the slice: x: 4 (x_hi: 2, x_lo: 2; x = x_hi * 2 + x_lo), y: 4, z: 16, core: 2. Of those that a mesh axis runs over, the one named last changes fastest.
Arguments:
- q_rows: bfloat16 [16384, 2560], P(('dp', 'seq'), 'head'), parts along dimension 0, may hold values from -6 to 6
- k_rows: bfloat16 [16384, 2560], P(('dp', 'seq'), 'head'), parts along dimension 0, may hold values from -6 to 6
- v_rows: bfloat16 [16384, 2560], P(('dp', 'seq'), 'head'), parts along dimension 0, may hold values from -6 to 6
- q_gain: float32 [2560], P('head'), may hold values from 0.8 to 2.5
- k_gain: float32 [2560], P('head'), may hold values from 0.8 to 2.5
- gate_table: float32 [50, 2560], P(None, 'head'), may hold values from 0.5 to 1.5
- clip_lengths: int32 [68], P('dp'), parts along dimension 0, may hold values from 1 to 512, 4096 in all
- clip_steps: int32 [68], P('dp'), parts along dimension 0, may hold values from 0 to 49
Outputs:
- attention_out: bfloat16 [16384, 2560], P(('dp', 'seq'), 'head'), parts along dimension 0
There are 4 independent parts, one for each index of `dp`. A program takes and returns all parts, laid end to end along the dimension named above; an argument that names none is the same for every part. Nothing has to cross between parts.
Inputs may be any that keep to these rules, and one draw needn't show every extreme that they name: `clip_lengths`: the lengths sum to 4096; the longest clip has exactly 512 tokens.
All inputs are finite; a program needn't handle non-finite values.
Results may differ from a plain program's by a relative error of at most 0.011.
Values may be sent and summed in bfloat16 or wider, within the bound.
No kernel may reach another device: no remote copies, remote signals or barrier semaphores. Data moves between devices by JAX's collectives and lax.ppermute only.
A program may use at most 64 MiB of HBM per device.

v0:
```python
import jax
import jax.numpy as jnp
from jax import lax
from jax.sharding import PartitionSpec as P

HEADS = 20
HD = 128
REACH = 4


def from_behind(value, axis, steps):
    count = lax.axis_size(axis)
    initial, last = (max(0, -steps), min(count, count - steps))
    return lax.ppermute(value, axis, [(source, source + steps) for source in range(initial, last)])


def clip_index(positions, ends):
    return jnp.sum((positions[:, None] >= ends[None, :]).astype(jnp.int32), axis=1)


def per_device(q_rows, k_rows, v_rows, q_gain, k_gain, gate_table, clip_lengths, clip_steps):
    rows, width = q_rows.shape
    heads_here = width // HD
    seq_index = lax.axis_index("seq")
    seq_count = lax.axis_size("seq")
    span = min(REACH, seq_count // 2)
    total_rows = rows * seq_count
    scale = HD ** (-0.5)
    q_data = q_rows.astype(jnp.float32)
    k_data = k_rows.astype(jnp.float32)
    square_q, square_k = lax.psum(
        (jnp.sum(q_data * q_data, axis=1), jnp.sum(k_data * k_data, axis=1)), "head"
    )
    features = HEADS * HD
    q_norm = (q_data * lax.rsqrt(square_q / features + 1e-06)[:, None] * q_gain[None, :]).astype(
        jnp.bfloat16
    )
    k_norm = (k_data * lax.rsqrt(square_k / features + 1e-06)[:, None] * k_gain[None, :]).astype(
        jnp.bfloat16
    )
    ends = jnp.cumsum(clip_lengths)
    positions = seq_index * rows + jnp.arange(rows, dtype=jnp.int32)
    row_clip = clip_index(positions, ends)
    picks = (
        row_clip[:, None] == jnp.arange(clip_lengths.shape[0], dtype=jnp.int32)[None, :]
    ).astype(jnp.int32)
    row_step = jnp.sum(picks * clip_steps[None, :], axis=1)
    table_pick = (
        row_step[:, None] == jnp.arange(gate_table.shape[0], dtype=jnp.int32)[None, :]
    ).astype(jnp.float32)
    gate_rows = jnp.dot(
        table_pick, gate_table, precision=lax.Precision.HIGHEST, preferred_element_type=jnp.float32
    )
    queries = q_norm.reshape(rows, heads_here, HD)
    bundle = jnp.stack([k_norm, v_rows])

    def attend(state, block, start):
        count = block.shape[1]
        key_pos = start + jnp.arange(count, dtype=jnp.int32)
        valid = (key_pos >= 0) & (key_pos < total_rows)
        key_clip = clip_index(key_pos, ends)
        highest, total, accum = state
        keys = block[0].reshape(count, heads_here, HD)
        values = block[1].reshape(count, heads_here, HD)
        scores = (
            jnp.einsum("qhd,khd->hqk", queries, keys, preferred_element_type=jnp.float32) * scale
        )
        mask = ((row_clip[:, None] == key_clip[None, :]) & valid[None, :])[None]
        scores = jnp.where(mask, scores, jnp.float32(-1e30))
        new_high = jnp.maximum(highest, jnp.max(scores, axis=-1))
        weights = jnp.where(mask, jnp.exp(scores - new_high[..., None]), jnp.float32(0.0))
        factor = jnp.exp(highest - new_high)
        total = total * factor + jnp.sum(weights, axis=-1)
        accum = accum * factor[..., None] + jnp.einsum(
            "hqk,khd->hqd", weights.astype(jnp.bfloat16), values, preferred_element_type=jnp.float32
        )
        return (new_high, total, accum)

    state = (
        jnp.full((heads_here, rows), -1e30, jnp.float32),
        jnp.zeros((heads_here, rows), jnp.float32),
        jnp.zeros((heads_here, rows, HD), jnp.float32),
    )
    state = attend(state, bundle, seq_index * rows)
    earlier = bundle
    later = bundle
    for distance in range(1, span + 1):
        earlier = from_behind(earlier, "seq", 1)
        state = attend(state, earlier, (seq_index - distance) * rows)
        later = from_behind(later, "seq", -1)
        state = attend(state, later, (seq_index + distance) * rows)
    highest, total, accum = state
    mixed = accum / total[..., None]
    mixed = jnp.transpose(mixed, (1, 0, 2)).reshape(rows, width)
    return (gate_rows * mixed).astype(jnp.bfloat16)


def solution(mesh):
    placed = (
        P(("dp", "seq"), "head"),
        P(("dp", "seq"), "head"),
        P(("dp", "seq"), "head"),
        P("head"),
        P("head"),
        P(None, "head"),
        P("dp"),
        P("dp"),
    )
    return jax.shard_map(
        per_device, mesh=mesh, in_specs=placed, out_specs=P(("dp", "seq"), "head"), check_vma=False
    )
```

profile of v0, /device:TPU:6, one launch (start us, length us, event | category | flops | bytes accessed | tf_op | source)
XLA Modules:
  0.0 82.7 jit_solution(2443480826450726518)
XLA Ops:
  0.0 1.1 %copy.74 = bf16[128,640]{0,1:T(8,128)(2,1)S(1)} copy(bf16[128,640]{1,0:T(8,128)(2,1)} %param.9) | data formatting | bytes 327680 | tf_op args[1]
  1.1 0.1 fusion.31
  1.2 0.8 copy-done.1
  2.0 0.2 copy.73
  2.2 0.1 fusion.28
  2.3 0.8 copy-done.2
  3.1 0.2 copy.77
  3.3 10.7 %all-reduce = (f32[128]{0:T(128)S(1)}, f32[128]{0:T(128)S(1)}) all-reduce(f32[128]{0:T(128)S(1)} %fusion.28, f32[128]{0:T(128)S(1)} %fusion.31), channel_id=1, replica_groups=mesh['seq'=32,'head'=4,'dp'=4] {'head'}, use_global_device_ids=true, to_apply=%region_4.0 | all-reduce | flops 256 | bytes 2048 | tf_op jit(solution)/shard_map/psum | solution.py:31
  14.1 0.7 copy-done.3
  14.7 0.1 fusion.159
  14.9 12.2 %collective-permute-start.1 = (bf16[2,128,640]{1,2,0:T(8,128)(2,1)S(1)}, bf16[2,128,640]{1,2,0:T(8,128)(2,1)S(1)}, u32[]{:S(2)}, u32[]{:S(2)}) collective-permute-start(bf16[2,128,640]{1,2,0:T(8,128)(2,1)S(1)} %pad_maximum_fusion), channel_id=1, source_target_pairs={{16,0},{32,16},{48,32},{64,48},{80,64},{96,80},{112,96},{128,112},... | collective-permute-start | bytes 983048 | tf_op jit(solution)/shard_map/ppermute | solution.py:14
  27.2 1.9 %collective-permute-start = (bf16[2,128,640]{1,2,0:T(8,128)(2,1)S(1)}, bf16[2,128,640]{1,2,0:T(8,128)(2,1)S(1)}, u32[]{:S(2)}, u32[]{:S(2)}) collective-permute-start(bf16[2,128,640]{1,2,0:T(8,128)(2,1)S(1)} %pad_maximum_fusion), channel_id=1, source_target_pairs={{0,16},{16,32},{32,48},{48,64},{64,80},{80,96},{96,112},{112,128},... | collective-permute-start | bytes 983048 | tf_op jit(solution)/shard_map/ppermute | solution.py:14
  29.3 0.2 fusion.33
  29.4 0.0 copy-start.5
  29.4 0.6 copy-done.5
  30.1 0.1 copy.72
  30.2 0.1 reduce
  30.3 0.5 copy-done.4
  30.9 0.1 fusion.30
  31.0 0.1 convert_reduce_fusion
  31.1 0.5 compare_and_fusion.6
  31.7 0.1 copy-done.6
  31.8 0.1 select_reduce_fusion
  31.9 0.3 fusion.130
  32.2 7.9 %collective-permute-start.3 = (bf16[2,128,640]{1,2,0:T(8,128)(2,1)S(1)}, bf16[2,128,640]{1,2,0:T(8,128)(2,1)S(1)}, u32[]{:S(2)}, u32[]{:S(2)}) collective-permute-start(bf16[2,128,640]{1,2,0:T(8,128)(2,1)S(1)} %collective-permute-done.1), channel_id=1, source_target_pairs={{16,0},{32,16},{48,32},{64,48},{80,64},{96,80},{112,96},{128,112},... | collective-permute-start | bytes 983048 | tf_op jit(solution)/shard_map/ppermute | solution.py:14
  40.1 0.3 fusion.128
  40.5 1.9 %collective-permute-start.2 = (bf16[2,128,640]{1,2,0:T(8,128)(2,1)S(1)}, bf16[2,128,640]{1,2,0:T(8,128)(2,1)S(1)}, u32[]{:S(2)}, u32[]{:S(2)}) collective-permute-start(bf16[2,128,640]{1,2,0:T(8,128)(2,1)S(1)} %collective-permute-done), channel_id=1, source_target_pairs={{0,16},{16,32},{32,48},{48,64},{64,80},{80,96},{96,112},{112,128},... | collective-permute-start | bytes 983048 | tf_op jit(solution)/shard_map/ppermute | solution.py:14
  42.4 0.3 fusion.129
  42.7 2.1 %collective-permute-done.3 = bf16[2,128,640]{1,2,0:T(8,128)(2,1)S(1)} collective-permute-done((bf16[2,128,640]{1,2,0:T(8,128)(2,1)S(1)}, bf16[2,128,640]{1,2,0:T(8,128)(2,1)S(1)}, u32[]{:S(2)}, u32[]{:S(2)}) %collective-permute-start.3) | collective-permute-done | bytes 327712 | tf_op jit(solution)/shard_map/ppermute | solution.py:14
  44.7 8.0 %collective-permute-start.5 = (bf16[2,128,640]{1,2,0:T(8,128)(2,1)S(1)}, bf16[2,128,640]{1,2,0:T(8,128)(2,1)S(1)}, u32[]{:S(2)}, u32[]{:S(2)}) collective-permute-start(bf16[2,128,640]{1,2,0:T(8,128)(2,1)S(1)} %collective-permute-done.3), channel_id=1, source_target_pairs={{16,0},{32,16},{48,32},{64,48},{80,64},{96,80},{112,96},{128,112},... | collective-permute-start | bytes 983048 | tf_op jit(solution)/shard_map/ppermute | solution.py:14
  52.7 0.3 fusion.126
  53.0 0.0 collective-permute-done.2
  53.1 0.3 fusion.127
  53.3 1.9 %collective-permute-start.4 = (bf16[2,128,640]{1,2,0:T(8,128)(2,1)S(1)}, bf16[2,128,640]{1,2,0:T(8,128)(2,1)S(1)}, u32[]{:S(2)}, u32[]{:S(2)}) collective-permute-start(bf16[2,128,640]{1,2,0:T(8,128)(2,1)S(1)} %collective-permute-done.2), channel_id=1, source_target_pairs={{0,16},{16,32},{32,48},{48,64},{64,80},{80,96},{96,112},{112,128},... | collective-permute-start | bytes 983048 | tf_op jit(solution)/shard_map/ppermute | solution.py:14
  55.3 2.0 %collective-permute-done.5 = bf16[2,128,640]{1,2,0:T(8,128)(2,1)S(1)} collective-permute-done((bf16[2,128,640]{1,2,0:T(8,128)(2,1)S(1)}, bf16[2,128,640]{1,2,0:T(8,128)(2,1)S(1)}, u32[]{:S(2)}, u32[]{:S(2)}) %collective-permute-start.5) | collective-permute-done | bytes 327712 | tf_op jit(solution)/shard_map/ppermute | solution.py:14
  57.3 8.0 %collective-permute-start.7 = (bf16[2,128,640]{1,2,0:T(8,128)(2,1)S(1)}, bf16[2,128,640]{1,2,0:T(8,128)(2,1)S(1)}, u32[]{:S(2)}, u32[]{:S(2)}) collective-permute-start(bf16[2,128,640]{1,2,0:T(8,128)(2,1)S(1)} %collective-permute-done.5), channel_id=1, source_target_pairs={{16,0},{32,16},{48,32},{64,48},{80,64},{96,80},{112,96},{128,112},... | collective-permute-start | bytes 983048 | tf_op jit(solution)/shard_map/ppermute | solution.py:14
  65.4 0.3 fusion.124
  65.6 0.3 collective-permute-done.4
  65.9 1.9 %collective-permute-start.6 = (bf16[2,128,640]{1,2,0:T(8,128)(2,1)S(1)}, bf16[2,128,640]{1,2,0:T(8,128)(2,1)S(1)}, u32[]{:S(2)}, u32[]{:S(2)}) collective-permute-start(bf16[2,128,640]{1,2,0:T(8,128)(2,1)S(1)} %collective-permute-done.4), channel_id=1, source_target_pairs={{0,16},{16,32},{32,48},{48,64},{64,80},{80,96},{96,112},{112,128},... | collective-permute-start | bytes 983048 | tf_op jit(solution)/shard_map/ppermute | solution.py:14
  67.9 0.3 fusion.125
  68.2 1.8 %collective-permute-done.7 = bf16[2,128,640]{1,2,0:T(8,128)(2,1)S(1)} collective-permute-done((bf16[2,128,640]{1,2,0:T(8,128)(2,1)S(1)}, bf16[2,128,640]{1,2,0:T(8,128)(2,1)S(1)}, u32[]{:S(2)}, u32[]{:S(2)}) %collective-permute-start.7) | collective-permute-done | bytes 327712 | tf_op jit(solution)/shard_map/ppermute | solution.py:14
  70.0 0.3 fusion.122
  70.2 8.3 %collective-permute-done.6 = bf16[2,128,640]{1,2,0:T(8,128)(2,1)S(1)} collective-permute-done((bf16[2,128,640]{1,2,0:T(8,128)(2,1)S(1)}, bf16[2,128,640]{1,2,0:T(8,128)(2,1)S(1)}, u32[]{:S(2)}, u32[]{:S(2)}) %collective-permute-start.6) | collective-permute-done | bytes 327712 | tf_op jit(solution)/shard_map/ppermute | solution.py:14
  78.6 0.3 fusion.123
  78.9 0.1 fusion.50
  78.9 0.1 fusion.48
  79.0 0.1 fusion.46
  79.1 0.1 fusion.44
  79.2 0.1 fusion.42
  79.3 0.1 fusion.40
  79.3 0.1 fusion.38
  79.4 0.1 fusion.36
  79.5 0.1 fusion.34
  79.6 0.2 fusion.26
  79.8 0.2 fusion.24
  80.0 0.2 fusion.22
  80.3 0.2 fusion.20
  80.5 0.2 fusion.18
  80.7 0.2 fusion.16
  80.9 0.2 fusion.14
  81.1 0.2 fusion.12
  81.3 0.2 fusion.10
  81.5 0.2 copy.104
  81.7 1.0 %fusion.27 = bf16[128,640]{1,0:T(8,128)(2,1)} fusion(f32[128,640]{1,0:T(8,128)S(1)} %copy.104, f32[50,640]{1,0:T(8,128)S(1)} %copy-done, s32[128]{0:T(128)S(1)} %select_reduce_fusion), kind=kOutput, calls=%fused_computation.46 | convolution fusion | flops 49322240 | bytes 620032 | tf_op jit(solution)/shard_map/dot_general | solution.py:51
  (33 shorter events, 0.4 us)
Async XLA Ops:
  0.0 81.7 %copy-start = (f32[50,640]{1,0:T(8,128)S(1)}, f32[50,640]{1,0:T(8,128)}, u32[]{:S(2)}) copy-start(f32[50,640]{1,0:T(8,128)} %param.13) | copy-start | bytes 384004
  1.1 0.9 %copy-start.1 = (bf16[128,640]{1,0:T(8,128)(2,1)S(1)}, bf16[128,640]{1,0:T(8,128)(2,1)}, u32[]{:S(2)}) copy-start(bf16[128,640]{1,0:T(8,128)(2,1)} %param.8) | copy-start | bytes 491524
  2.2 0.9 %copy-start.2 = (bf16[128,640]{1,0:T(8,128)(2,1)S(1)}, bf16[128,640]{1,0:T(8,128)(2,1)}, u32[]{:S(2)}) copy-start(bf16[128,640]{1,0:T(8,128)(2,1)} %param.10) | copy-start | bytes 491524
  14.0 0.7 copy-start.3
  14.9 17.2 %collective-permute-start.1 = (bf16[2,128,640]{1,2,0:T(8,128)(2,1)S(1)}, bf16[2,128,640]{1,2,0:T(8,128)(2,1)S(1)}, u32[]{:S(2)}, u32[]{:S(2)}) collective-permute-start(bf16[2,128,640]{1,2,0:T(8,128)(2,1)S(1)} %pad_maximum_fusion), channel_id=1, source_target_pairs={{16,0},{32,16},{48,32},{64,48},{80,64},{96,80},{112,96},{128,112},... | collective-permute-start | bytes 983048 | tf_op jit(solution)/shard_map/ppermute | solution.py:14
  27.2 13.2 %collective-permute-start = (bf16[2,128,640]{1,2,0:T(8,128)(2,1)S(1)}, bf16[2,128,640]{1,2,0:T(8,128)(2,1)S(1)}, u32[]{:S(2)}, u32[]{:S(2)}) collective-permute-start(bf16[2,128,640]{1,2,0:T(8,128)(2,1)S(1)} %pad_maximum_fusion), channel_id=1, source_target_pairs={{0,16},{16,32},{32,48},{48,64},{64,80},{80,96},{96,112},{112,128},... | collective-permute-start | bytes 983048 | tf_op jit(solution)/shard_map/ppermute | solution.py:14
  29.4 0.7 copy-start.5
  30.2 0.7 copy-start.4
  31.1 0.7 copy-start.6
  32.2 12.5 %collective-permute-start.3 = (bf16[2,128,640]{1,2,0:T(8,128)(2,1)S(1)}, bf16[2,128,640]{1,2,0:T(8,128)(2,1)S(1)}, u32[]{:S(2)}, u32[]{:S(2)}) collective-permute-start(bf16[2,128,640]{1,2,0:T(8,128)(2,1)S(1)} %collective-permute-done.1), channel_id=1, source_target_pairs={{16,0},{32,16},{48,32},{64,48},{80,64},{96,80},{112,96},{128,112},... | collective-permute-start | bytes 983048 | tf_op jit(solution)/shard_map/ppermute | solution.py:14
  40.5 12.6 %collective-permute-start.2 = (bf16[2,128,640]{1,2,0:T(8,128)(2,1)S(1)}, bf16[2,128,640]{1,2,0:T(8,128)(2,1)S(1)}, u32[]{:S(2)}, u32[]{:S(2)}) collective-permute-start(bf16[2,128,640]{1,2,0:T(8,128)(2,1)S(1)} %collective-permute-done), channel_id=1, source_target_pairs={{0,16},{16,32},{32,48},{48,64},{64,80},{80,96},{96,112},{112,128},... | collective-permute-start | bytes 983048 | tf_op jit(solution)/shard_map/ppermute | solution.py:14
  44.7 12.6 %collective-permute-start.5 = (bf16[2,128,640]{1,2,0:T(8,128)(2,1)S(1)}, bf16[2,128,640]{1,2,0:T(8,128)(2,1)S(1)}, u32[]{:S(2)}, u32[]{:S(2)}) collective-permute-start(bf16[2,128,640]{1,2,0:T(8,128)(2,1)S(1)} %collective-permute-done.3), channel_id=1, source_target_pairs={{16,0},{32,16},{48,32},{64,48},{80,64},{96,80},{112,96},{128,112},... | collective-permute-start | bytes 983048 | tf_op jit(solution)/shard_map/ppermute | solution.py:14
  53.3 12.6 %collective-permute-start.4 = (bf16[2,128,640]{1,2,0:T(8,128)(2,1)S(1)}, bf16[2,128,640]{1,2,0:T(8,128)(2,1)S(1)}, u32[]{:S(2)}, u32[]{:S(2)}) collective-permute-start(bf16[2,128,640]{1,2,0:T(8,128)(2,1)S(1)} %collective-permute-done.2), channel_id=1, source_target_pairs={{0,16},{16,32},{32,48},{48,64},{64,80},{80,96},{96,112},{112,128},... | collective-permute-start | bytes 983048 | tf_op jit(solution)/shard_map/ppermute | solution.py:14
  57.3 12.6 %collective-permute-start.7 = (bf16[2,128,640]{1,2,0:T(8,128)(2,1)S(1)}, bf16[2,128,640]{1,2,0:T(8,128)(2,1)S(1)}, u32[]{:S(2)}, u32[]{:S(2)}) collective-permute-start(bf16[2,128,640]{1,2,0:T(8,128)(2,1)S(1)} %collective-permute-done.5), channel_id=1, source_target_pairs={{16,0},{32,16},{48,32},{64,48},{80,64},{96,80},{112,96},{128,112},... | collective-permute-start | bytes 983048 | tf_op jit(solution)/shard_map/ppermute | solution.py:14
  65.9 12.6 %collective-permute-start.6 = (bf16[2,128,640]{1,2,0:T(8,128)(2,1)S(1)}, bf16[2,128,640]{1,2,0:T(8,128)(2,1)S(1)}, u32[]{:S(2)}, u32[]{:S(2)}) collective-permute-start(bf16[2,128,640]{1,2,0:T(8,128)(2,1)S(1)} %collective-permute-done.4), channel_id=1, source_target_pairs={{0,16},{16,32},{32,48},{48,64},{64,80},{80,96},{96,112},{112,128},... | collective-permute-start | bytes 983048 | tf_op jit(solution)/shard_map/ppermute | solution.py:14
where the time goes:
time: 83.1 us; the launch traced here: 82.7 us
  starting transfers between devices  43.9 us (53%)
  waiting for transfers between devices  14.5 us (17%)
  blocking collectives  10.7 us (13%)
  local copies, waits for them, and re-layouts  5.48 us (7%)
  matrix products  5.29 us (6%)
  other arithmetic  2.36 us (3%)
    ppermute x8, starting transfers between devices, from_behind(): lax.ppermute(value, axis, [(source, source + steps) for source in range(i...  43.9 us
    ppermute x8, waiting for transfers between devices, from_behind(): lax.ppermute(value, axis, [(source, source + steps) for source in range(i...  14.5 us
    psum x1, blocking collectives, per_device(): lax.psum((jnp.sum(q_data * q_data, axis=1), jnp.sum(k_data * k_data, axis...  10.7 us
    unnamed x17, local copies, waits for them, and re-layouts  5.04 us
    dot_general x9, matrix products, attend(): jnp.einsum('qhd,khd->hqk', queries, keys, preferred_element_type=jnp.floa...  2.45 us
    dot_general x9, matrix products, attend(): jnp.einsum('hqk,khd->hqd', weights.astype(jnp.bfloat16), values, preferre...  1.84 us
  transfers between devices with their start and end apart: 8, of which 5 were waited for; matrix products, arithmetic and copies ran while one was open for 4% of the time, Pallas kernels for 0%

commit v1 on v0

v1 whole, which is shorter than its diff:
```python
import functools
import math

import jax
import jax.numpy as jnp
from jax import lax
from jax.experimental import pallas as pl
from jax.experimental.pallas import tpu as pltpu
from jax.sharding import PartitionSpec as P

HEADS = 20
HD = 128
FAR = 3
LOW = -1e30
SCALE2 = HD ** (-0.5) * math.log2(math.e)
EXTRA = 16


def shifted(value, steps):
    count = lax.axis_size("seq")
    return lax.ppermute(value, "seq", [(source, (source + steps) % count) for source in range(count)])


def eye(size):
    return lax.broadcasted_iota(jnp.int32, (size, size), 0) == lax.broadcasted_iota(jnp.int32, (size, size), 1)


def as_row(column):
    size = column.shape[0]
    return jnp.sum(jnp.where(eye(size), column, 0.0), axis=0, keepdims=True)


def as_column(row):
    size = row.shape[1]
    return jnp.sum(jnp.where(eye(size), row, 0.0), axis=1, keepdims=True)


def clip_of(positions, lengths_ref):
    end = lengths_ref[0]
    found = (positions >= end).astype(jnp.int32)
    for clip in range(1, lengths_ref.shape[0]):
        end = end + lengths_ref[clip]
        found = found + (positions >= end).astype(jnp.int32)
    return found


def neighbour(place_ref, step):
    block, count = place_ref[0] + step, place_ref[1]
    return jnp.where(block < 0, block + count, jnp.where(block >= count, block - count, block))


def row_clips(block, rows, lengths_ref):
    return clip_of(block * rows + lax.broadcasted_iota(jnp.int32, (rows, 1), 0), lengths_ref)


def key_clips(block, rows, lengths_ref):
    return clip_of(block * rows + lax.broadcasted_iota(jnp.int32, (1, rows), 1), lengths_ref)


def squares_kernel(q_ref, k_ref, out_ref):
    def total(ref):
        data = ref[...].astype(jnp.float32)
        return as_row(jnp.sum(data * data, axis=1, keepdims=True))

    rows = out_ref.shape[2]
    both = jnp.concatenate([total(q_ref), total(k_ref), jnp.zeros((6, rows), jnp.float32)], axis=0)
    for peer in range(out_ref.shape[0]):
        out_ref[peer] = both


def norm_kernel(squares_ref, q_ref, k_ref, q_gain_ref, k_gain_ref, q_out, k_out):
    both = squares_ref[0]
    for peer in range(1, squares_ref.shape[0]):
        both = both + squares_ref[peer]
    factors = lax.rsqrt(both / (HEADS * HD) + 1e-06)
    for line, (ref, gain_ref, out) in enumerate([(q_ref, q_gain_ref, q_out), (k_ref, k_gain_ref, k_out)]):
        scaled = ref[...].astype(jnp.float32) * as_column(factors[line : line + 1])
        out[...] = (scaled * gain_ref[...]).astype(jnp.bfloat16)


def attend(queries, keys, values, masks):
    scores = [
        jnp.where(mask, lax.dot_general(queries, key, (((1,), (1,)), ((), ())), preferred_element_type=jnp.float32), LOW)
        for key, mask in zip(keys, masks)
    ]
    highest = jnp.max(functools.reduce(jnp.maximum, scores), axis=1, keepdims=True)
    weights = [jnp.exp2((score - highest) * SCALE2) for score in scores]
    total = jnp.sum(functools.reduce(jnp.add, weights), axis=1, keepdims=True)
    mixed = functools.reduce(
        jnp.add,
        [
            jnp.dot(weight.astype(jnp.bfloat16), value, preferred_element_type=jnp.float32)
            for weight, value in zip(weights, values)
        ],
    )
    return mixed / total, highest * SCALE2 + jnp.log2(total)


def guest_kernel(place_ref, lengths_ref, ql, qr, kl, km, kr, vl, vm, vr, left_out, right_out):
    rows, width = ql.shape
    key_ids = [key_clips(neighbour(place_ref, step), rows, lengths_ref) for step in (-FAR, 0, FAR)]
    for queries_ref, step, out in ((ql, -1, left_out), (qr, 1, right_out)):
        query_ids = row_clips(neighbour(place_ref, step), rows, lengths_ref)
        masks = [query_ids == ids for ids in key_ids]
        out[rows:, :] = jnp.zeros((EXTRA, width), jnp.bfloat16)
        for head in range(width // HD):
            at = slice(head * HD, (head + 1) * HD)
            mixed, level = attend(
                queries_ref[:, at], [ref[:, at] for ref in (kl, km, kr)], [ref[:, at] for ref in (vl, vm, vr)], masks
            )
            out[:rows, at] = mixed.astype(jnp.bfloat16)
            rest = as_row(level)
            lines = []
            for _ in range(3):
                piece = rest.astype(jnp.bfloat16)
                rest = rest - piece.astype(jnp.float32)
                lines.append(piece.astype(jnp.float32))
            pad = jnp.zeros((EXTRA - 3, rows), jnp.float32)
            out[rows:, at] = jnp.concatenate(lines + [pad], axis=0).astype(jnp.bfloat16)


def home_kernel(place_ref, lengths_ref, steps_ref, table, q, kl, km, kr, vl, vm, vr, mixed_out, level_out, gate_out):
    rows, width = q.shape
    query_ids = row_clips(place_ref[0], rows, lengths_ref)
    masks = [query_ids == key_clips(neighbour(place_ref, step), rows, lengths_ref) for step in (-FAR, 0, FAR)]
    levels = []
    for head in range(width // HD):
        at = slice(head * HD, (head + 1) * HD)
        mixed, level = attend(q[:, at], [ref[:, at] for ref in (kl, km, kr)], [ref[:, at] for ref in (vl, vm, vr)], masks)
        mixed_out[:, at] = mixed
        levels.append(jnp.broadcast_to(level, (rows, HD)))
    for head, level in enumerate(levels):
        level_out[:, head * HD : (head + 1) * HD] = level
    gate = jnp.zeros((rows, width), jnp.float32)
    for clip in range(lengths_ref.shape[0]):
        gate = jnp.where(query_ids == clip, table[pl.ds(steps_ref[clip], 1), :], gate)
    gate_out[...] = gate


def join_kernel(gate, mixed, levels, from_left, from_right, out):
    rows, width = mixed.shape
    for head in range(width // HD):
        at = slice(head * HD, (head + 1) * HD)
        parts = [(levels[:, at], mixed[:, at])]
        for ref in (from_left, from_right):
            lines = ref[rows:, at].astype(jnp.float32)
            level = as_column(lines[0:1] + lines[1:2] + lines[2:3])
            parts.append((level, ref[:rows, at].astype(jnp.float32)))
        top = functools.reduce(jnp.maximum, [level for level, _ in parts])
        shares = [jnp.exp2(level - top) for level, _ in parts]
        total = functools.reduce(jnp.add, shares)
        joined = functools.reduce(jnp.add, [share * part for share, (_, part) in zip(shares, parts)])
        out[:, at] = (gate[:, at] * joined / total).astype(jnp.bfloat16)


def call(kernel, outs, scalars, arrays, flops=0):
    space = [pl.BlockSpec(memory_space=pltpu.SMEM)] * len(scalars) + [pl.BlockSpec(memory_space=pltpu.VMEM)] * len(arrays)
    size = sum(math.prod(a.shape) * a.dtype.itemsize for a in list(arrays) + list(outs))
    return pl.pallas_call(
        kernel,
        out_shape=outs,
        in_specs=space,
        out_specs=[pl.BlockSpec(memory_space=pltpu.VMEM)] * len(outs),
        compiler_params=pltpu.CompilerParams(vmem_limit_bytes=32 * 2**20),
        cost_estimate=pl.CostEstimate(flops=flops, bytes_accessed=size, transcendentals=0),
    )(*scalars, *arrays)


def per_device(q_rows, k_rows, v_rows, q_gain, k_gain, gate_table, clip_lengths, clip_steps):
    rows, width = q_rows.shape
    heads_here = width // HD
    peers = lax.axis_size("head")
    place = jnp.stack([lax.axis_index("seq"), lax.axis_size("seq")]).astype(jnp.int32)
    bf16 = functools.partial(jax.ShapeDtypeStruct, dtype=jnp.bfloat16)
    f32 = functools.partial(jax.ShapeDtypeStruct, dtype=jnp.float32)

    v_left, v_right = shifted(v_rows, FAR), shifted(v_rows, -FAR)
    (squares,) = call(squares_kernel, [f32((peers, 8, rows))], [], [q_rows, k_rows])
    squares = lax.all_to_all(squares, "head", 0, 0)
    q_norm, k_norm = call(
        norm_kernel,
        [bf16((rows, width)), bf16((rows, width))],
        [],
        [squares, q_rows, k_rows, q_gain.reshape(1, width), k_gain.reshape(1, width)],
    )
    k_left, k_right = shifted(k_norm, FAR), shifted(k_norm, -FAR)
    q_left, q_right = shifted(q_norm, 1), shifted(q_norm, -1)
    around = [k_left, k_norm, k_right, v_left, v_rows, v_right]
    flops = 4 * rows * 3 * rows * HD * heads_here
    to_left, to_right = call(
        guest_kernel,
        [bf16((rows + EXTRA, width))] * 2,
        [place, clip_lengths],
        [q_left, q_right] + around,
        2 * flops,
    )
    from_right, from_left = shifted(to_left, -1), shifted(to_right, 1)
    mixed, levels, gate = call(
        home_kernel,
        [f32((rows, width))] * 3,
        [place, clip_lengths, clip_steps],
        [gate_table, q_norm] + around,
        flops,
    )
    (out,) = call(
        join_kernel, [bf16((rows, width))], [], [gate, mixed, levels, from_left, from_right]
    )
    return out


def solution(mesh):
    placed = (
        P(("dp", "seq"), "head"),
        P(("dp", "seq"), "head"),
        P(("dp", "seq"), "head"),
        P("head"),
        P("head"),
        P(None, "head"),
        P("dp"),
        P("dp"),
    )
    return jax.shard_map(
        per_device, mesh=mesh, in_specs=placed, out_specs=P(("dp", "seq"), "head"), check_vma=False
    )
```

time: 83.1 us -> 68.5 us (0.82)
  the two profiles are of different devices: /device:TPU:6 before, /device:TPU:8 now
where the time goes in v1:
time: 68.5 us; the launch traced here: 68.1 us
  starting transfers between devices  52.5 us (77%)
  Pallas kernels  7.95 us (12%)
  waiting for transfers between devices  5.52 us (8%)
  local copies, waits for them, and re-layouts  1.87 us (3%)
    ppermute x8, starting transfers between devices, shifted(): lax.ppermute(value, 'seq', [(source, (source + steps) % count) for source...  47.4 us
    pallas_call x5, Pallas kernels, call(): pl.pallas_call(kernel, out_shape=outs, in_specs=space, out_specs=[pl.Bloc...  7.95 us
    ppermute x8, waiting for transfers between devices, shifted(): lax.ppermute(value, 'seq', [(source, (source + steps) % count) for source...  5.52 us
    all_to_all x1, starting transfers between devices, per_device(): squares = lax.all_to_all(squares, 'head', 0, 0)  5.04 us
    unnamed x20, local copies, waits for them, and re-layouts  1.86 us
  transfers between devices with their start and end apart: 9, of which 3 were waited for; matrix products, arithmetic and copies ran while one was open for 0% of the time, Pallas kernels for 5%

profile of v1, /device:TPU:8, one launch (start us, length us, event | category | flops | bytes accessed | tf_op | source)
XLA Modules:
  0.0 68.1 jit_solution(18277690868032068178)
XLA Ops:
  0.0 6.5 %collective-permute-start.2 = (bf16[128,640]{1,0:T(8,128)(2,1)}, bf16[128,640]{1,0:T(8,128)(2,1)S(1)}, u32[]{:S(2)}, u32[]{:S(2)}) collective-permute-start(bf16[128,640]{1,0:T(8,128)(2,1)} %vm.3), channel_id=1, source_target_pairs={{0,48},{16,64},{32,80},{48,96},{64,112},{80,128},{96,144},{112,160... | collective-permute-start | bytes 491528 | tf_op jit(solution)/shard_map/ppermute | solution.py:21
  6.5 0.0 copy-start
  6.5 0.9 %copy-done = bf16[128,640]{1,0:T(8,128)(2,1)S(1)} copy-done((bf16[128,640]{1,0:T(8,128)(2,1)S(1)}, bf16[128,640]{1,0:T(8,128)(2,1)}, u32[]{:S(2)}) %copy-start) | copy-done | bytes 163864
  7.4 0.0 copy-start.2
  7.5 0.9 %copy-done.2 = bf16[128,640]{1,0:T(8,128)(2,1)S(1)} copy-done((bf16[128,640]{1,0:T(8,128)(2,1)S(1)}, bf16[128,640]{1,0:T(8,128)(2,1)}, u32[]{:S(2)}) %copy-start.2) | copy-done | bytes 163864
  8.4 0.0 copy-start.1
  8.4 0.0 copy-start.3
  8.4 0.8 %shard_map.82 = f32[4,8,128]{2,1,0:T(8,128)} custom-call(bf16[128,640]{1,0:T(8,128)(2,1)S(1)} %copy-done, bf16[128,640]{1,0:T(8,128)(2,1)S(1)} %copy-done.2), custom_call_target="tpu_custom_call" | custom-call | bytes 344064 | tf_op jit(solution)/shard_map/pallas_call | solution.py:159
  9.1 0.0 copy-start.8
  9.1 5.0 %all-to-all-start = ((f32[4,8,128]{2,1,0:T(8,128)}), f32[4,8,128]{2,1,0:T(8,128)S(1)}, u32[]{:S(2)}, u32[]{:S(2)}) async-start(f32[4,8,128]{2,1,0:T(8,128)} %shard_map.82), calls=%async_computation | async-start | bytes 32768 | tf_op jit(solution)/shard_map/all_to_all | solution.py:179
  14.2 0.0 copy-start.9
  14.2 10.3 %collective-permute-start.3 = (bf16[128,640]{1,0:T(8,128)(2,1)}, bf16[128,640]{1,0:T(8,128)(2,1)S(1)}, u32[]{:S(2)}, u32[]{:S(2)}) collective-permute-start(bf16[128,640]{1,0:T(8,128)(2,1)} %vm.3), channel_id=1, source_target_pairs={{0,464},{16,480},{32,496},{48,0},{64,16},{80,32},{96,48},{112,64},... | collective-permute-start | bytes 491528 | tf_op jit(solution)/shard_map/ppermute | solution.py:21
  24.4 0.0 copy-done.8
  24.5 0.0 copy-done.9
  24.5 0.0 copy-start.4
  24.5 0.0 all-to-all-done.squares_ref
  24.5 0.0 copy-done.1
  24.5 0.0 copy-done.3
  24.5 0.2 shard_map.83
  24.7 1.9 %collective-permute-start = (bf16[128,640]{1,0:T(8,128)(2,1)S(1)}, bf16[128,640]{1,0:T(8,128)(2,1)S(1)}, u32[]{:S(2)}, u32[]{:S(2)}) collective-permute-start(bf16[128,640]{1,0:T(8,128)(2,1)S(1)} %get-tuple-element.13.km), channel_id=1, source_target_pairs={{0,48},{16,64},{32,80},{48,96},{64,112},{80,128},{96,144},{112,160... | collective-permute-start | bytes 491528 | tf_op jit(solution)/shard_map/ppermute | solution.py:21
  26.6 9.3 %collective-permute-start.1 = (bf16[128,640]{1,0:T(8,128)(2,1)S(1)}, bf16[128,640]{1,0:T(8,128)(2,1)S(1)}, u32[]{:S(2)}, u32[]{:S(2)}) collective-permute-start(bf16[128,640]{1,0:T(8,128)(2,1)S(1)} %get-tuple-element.13.km), channel_id=1, source_target_pairs={{0,464},{16,480},{32,496},{48,0},{64,16},{80,32},{96,48},{112,64},... | collective-permute-start | bytes 491528 | tf_op jit(solution)/shard_map/ppermute | solution.py:21
  36.0 2.9 %collective-permute-start.4 = (bf16[128,640]{1,0:T(8,128)(2,1)S(1)}, bf16[128,640]{1,0:T(8,128)(2,1)S(1)}, u32[]{:S(2)}, u32[]{:S(2)}) collective-permute-start(bf16[128,640]{1,0:T(8,128)(2,1)S(1)} %get-tuple-element.12.q), channel_id=1, source_target_pairs={{0,16},{16,32},{32,48},{48,64},{64,80},{80,96},{96,112},{112,128},... | collective-permute-start | bytes 491528 | tf_op jit(solution)/shard_map/ppermute | solution.py:21
  38.9 0.0 collective-permute-done.2.vl
  38.9 6.5 %collective-permute-start.5 = (bf16[128,640]{1,0:T(8,128)(2,1)S(1)}, bf16[128,640]{1,0:T(8,128)(2,1)S(1)}, u32[]{:S(2)}, u32[]{:S(2)}) collective-permute-start(bf16[128,640]{1,0:T(8,128)(2,1)S(1)} %get-tuple-element.12.q), channel_id=1, source_target_pairs={{0,496},{16,0},{32,16},{48,32},{64,48},{80,64},{96,80},{112,96},{1... | collective-permute-start | bytes 491528 | tf_op jit(solution)/shard_map/ppermute | solution.py:21
  45.5 0.0 copy-start.6
  45.5 0.1 pad_add_fusion.place_ref
  45.5 0.0 copy-start.5
  45.5 0.0 collective-permute-done.3.vr
  45.5 0.0 collective-permute-done.kl
  45.6 1.6 %collective-permute-done.1.kr = bf16[128,640]{1,0:T(8,128)(2,1)S(1)} collective-permute-done((bf16[128,640]{1,0:T(8,128)(2,1)S(1)}, bf16[128,640]{1,0:T(8,128)(2,1)S(1)}, u32[]{:S(2)}, u32[]{:S(2)}) %collective-permute-start.1) | collective-permute-done | bytes 163872 | tf_op jit(solution)/shard_map/ppermute | solution.py:21
  47.1 0.0 collective-permute-done.4.ql
  47.2 2.8 %collective-permute-done.5.qr = bf16[128,640]{1,0:T(8,128)(2,1)S(1)} collective-permute-done((bf16[128,640]{1,0:T(8,128)(2,1)S(1)}, bf16[128,640]{1,0:T(8,128)(2,1)S(1)}, u32[]{:S(2)}, u32[]{:S(2)}) %collective-permute-start.5) | collective-permute-done | bytes 163872 | tf_op jit(solution)/shard_map/ppermute | solution.py:21
  50.0 0.0 copy-done.4
  50.0 0.0 copy-done.6
  50.0 3.6 %shard_map.85 = (bf16[144,640]{1,0:T(8,128)(2,1)S(1)}, bf16[144,640]{1,0:T(8,128)(2,1)S(1)}) custom-call(s32[2]{0:T(128)S(1)} %pad_add_fusion.place_ref, s32[17]{0:T(128)S(1)} %copy-done.6, bf16[128,640]{1,0:T(8,128)(2,1)S(1)} %collective-permute-done.4.ql, bf16[128,640]{1,0:T(8,128)(2,1)S(1)} %collective-permute-done.5.qr, ...), custom_call_target="tpu_custom_call" | custom-call | flops 251658240 | bytes 1679360 | tf_op jit(solution)/shard_map/pallas_call | solution.py:159
  53.6 0.0 copy-start.7
  53.6 1.9 %collective-permute-start.6 = (bf16[144,640]{1,0:T(8,128)(2,1)S(1)}, bf16[144,640]{1,0:T(8,128)(2,1)S(1)}, u32[]{:S(2)}, u32[]{:S(2)}) collective-permute-start(bf16[144,640]{1,0:T(8,128)(2,1)S(1)} %get-tuple-element.17), channel_id=1, source_target_pairs={{0,16},{16,32},{32,48},{48,64},{64,80},{80,96},{96,112},{112,128},... | collective-permute-start | bytes 552968 | tf_op jit(solution)/shard_map/ppermute | solution.py:21
  55.6 8.0 %collective-permute-start.7 = (bf16[144,640]{1,0:T(8,128)(2,1)S(1)}, bf16[144,640]{1,0:T(8,128)(2,1)S(1)}, u32[]{:S(2)}, u32[]{:S(2)}) collective-permute-start(bf16[144,640]{1,0:T(8,128)(2,1)S(1)} %get-tuple-element.18), channel_id=1, source_target_pairs={{0,496},{16,0},{32,16},{48,32},{64,48},{80,64},{96,80},{112,96},{1... | collective-permute-start | bytes 552968 | tf_op jit(solution)/shard_map/ppermute | solution.py:21
  63.6 0.0 copy-done.5
  63.6 0.0 copy-done.7
  63.6 2.4 %shard_map.84 = (f32[128,640]{1,0:T(8,128)S(1)}, f32[128,640]{1,0:T(8,128)S(1)}, f32[128,640]{1,0:T(8,128)S(1)}) custom-call(s32[2]{0:T(128)S(1)} %pad_add_fusion.place_ref, s32[17]{0:T(128)S(1)} %copy-done.6, s32[17]{0:T(128)S(1)} %copy-done.7, f32[50,640]{1,0:T(8,128)S(1)} %copy-done.5, bf16[128,640]{1,0:T(8,128)(2,1)S(1)} %get-tuple-element.12.q, ...), custom_call_target="tpu_custom_call" | custom-call | flops 125829120 | bytes 2257920 | tf_op jit(solution)/shard_map/pallas_call | solution.py:159
  66.0 0.0 collective-permute-done.6.from_left
  66.0 1.1 %collective-permute-done.7.from_right = bf16[144,640]{1,0:T(8,128)(2,1)S(1)} collective-permute-done((bf16[144,640]{1,0:T(8,128)(2,1)S(1)}, bf16[144,640]{1,0:T(8,128)(2,1)S(1)}, u32[]{:S(2)}, u32[]{:S(2)}) %collective-permute-start.7) | collective-permute-done | bytes 184352 | tf_op jit(solution)/shard_map/ppermute | solution.py:21
  67.1 1.0 %shard_map.86 = bf16[128,640]{1,0:T(8,128)(2,1)} custom-call(f32[128,640]{1,0:T(8,128)S(1)} %get-tuple-element.14.gate, f32[128,640]{1,0:T(8,128)S(1)} %get-tuple-element.15.mixed, f32[128,640]{1,0:T(8,128)S(1)} %get-tuple-element.16.levels, bf16[144,640]{1,0:T(8,128)(2,1)S(1)} %collective-permute-done.6.from_left, ...), custom_call_target="tpu_custom_call" | custom-call | bytes 1515520 | tf_op jit(solution)/shard_map/pallas_call | solution.py:159
  (2 shorter events, 0.0 us)
Async XLA Ops:
  0.0 38.9 %collective-permute-start.2 = (bf16[128,640]{1,0:T(8,128)(2,1)}, bf16[128,640]{1,0:T(8,128)(2,1)S(1)}, u32[]{:S(2)}, u32[]{:S(2)}) collective-permute-start(bf16[128,640]{1,0:T(8,128)(2,1)} %vm.3), channel_id=1, source_target_pairs={{0,48},{16,64},{32,80},{48,96},{64,112},{80,128},{96,144},{112,160... | collective-permute-start | bytes 491528 | tf_op jit(solution)/shard_map/ppermute | solution.py:21
  6.5 0.9 %copy-start = (bf16[128,640]{1,0:T(8,128)(2,1)S(1)}, bf16[128,640]{1,0:T(8,128)(2,1)}, u32[]{:S(2)}) copy-start(bf16[128,640]{1,0:T(8,128)(2,1)} %q_ref.3) | copy-start | bytes 491524
  7.4 0.9 %copy-start.2 = (bf16[128,640]{1,0:T(8,128)(2,1)S(1)}, bf16[128,640]{1,0:T(8,128)(2,1)}, u32[]{:S(2)}) copy-start(bf16[128,640]{1,0:T(8,128)(2,1)} %k_ref.3) | copy-start | bytes 491524
  8.4 16.1 %copy-start.1 = (bf16[128,640]{1,0:T(8,128)(2,1)S(1)}, bf16[128,640]{1,0:T(8,128)(2,1)}, u32[]{:S(2)}) copy-start(bf16[128,640]{1,0:T(8,128)(2,1)} %q_ref.3) | copy-start | bytes 491524
  8.4 16.1 %copy-start.3 = (bf16[128,640]{1,0:T(8,128)(2,1)S(1)}, bf16[128,640]{1,0:T(8,128)(2,1)}, u32[]{:S(2)}) copy-start(bf16[128,640]{1,0:T(8,128)(2,1)} %k_ref.3) | copy-start | bytes 491524
  9.1 15.3 %copy-start.8 = (f32[640]{0:T(1024)S(1)}, f32[640]{0:T(1024)}, u32[]{:S(2)}) copy-start(f32[640]{0:T(1024)} %param.11) | copy-start | bytes 7684
  9.1 15.4 %all-to-all-start = ((f32[4,8,128]{2,1,0:T(8,128)}), f32[4,8,128]{2,1,0:T(8,128)S(1)}, u32[]{:S(2)}, u32[]{:S(2)}) async-start(f32[4,8,128]{2,1,0:T(8,128)} %shard_map.82), calls=%async_computation | async-start | bytes 32768 | tf_op jit(solution)/shard_map/all_to_all | solution.py:179
  14.2 10.3 %copy-start.9 = (f32[640]{0:T(1024)S(1)}, f32[640]{0:T(1024)}, u32[]{:S(2)}) copy-start(f32[640]{0:T(1024)} %param.12) | copy-start | bytes 7684
  14.2 31.4 %collective-permute-start.3 = (bf16[128,640]{1,0:T(8,128)(2,1)}, bf16[128,640]{1,0:T(8,128)(2,1)S(1)}, u32[]{:S(2)}, u32[]{:S(2)}) collective-permute-start(bf16[128,640]{1,0:T(8,128)(2,1)} %vm.3), channel_id=1, source_target_pairs={{0,464},{16,480},{32,496},{48,0},{64,16},{80,32},{96,48},{112,64},... | collective-permute-start | bytes 491528 | tf_op jit(solution)/shard_map/ppermute | solution.py:21
  24.5 25.5 %copy-start.4 = (bf16[128,640]{1,0:T(8,128)(2,1)S(1)}, bf16[128,640]{1,0:T(8,128)(2,1)}, u32[]{:S(2)}) copy-start(bf16[128,640]{1,0:T(8,128)(2,1)} %vm.3) | copy-start | bytes 491524
  24.7 20.9 %collective-permute-start = (bf16[128,640]{1,0:T(8,128)(2,1)S(1)}, bf16[128,640]{1,0:T(8,128)(2,1)S(1)}, u32[]{:S(2)}, u32[]{:S(2)}) collective-permute-start(bf16[128,640]{1,0:T(8,128)(2,1)S(1)} %get-tuple-element.13.km), channel_id=1, source_target_pairs={{0,48},{16,64},{32,80},{48,96},{64,112},{80,128},{96,144},{112,160... | collective-permute-start | bytes 491528 | tf_op jit(solution)/shard_map/ppermute | solution.py:21
  26.6 20.5 %collective-permute-start.1 = (bf16[128,640]{1,0:T(8,128)(2,1)S(1)}, bf16[128,640]{1,0:T(8,128)(2,1)S(1)}, u32[]{:S(2)}, u32[]{:S(2)}) collective-permute-start(bf16[128,640]{1,0:T(8,128)(2,1)S(1)} %get-tuple-element.13.km), channel_id=1, source_target_pairs={{0,464},{16,480},{32,496},{48,0},{64,16},{80,32},{96,48},{112,64},... | collective-permute-start | bytes 491528 | tf_op jit(solution)/shard_map/ppermute | solution.py:21
  36.0 11.2 %collective-permute-start.4 = (bf16[128,640]{1,0:T(8,128)(2,1)S(1)}, bf16[128,640]{1,0:T(8,128)(2,1)S(1)}, u32[]{:S(2)}, u32[]{:S(2)}) collective-permute-start(bf16[128,640]{1,0:T(8,128)(2,1)S(1)} %get-tuple-element.12.q), channel_id=1, source_target_pairs={{0,16},{16,32},{32,48},{48,64},{64,80},{80,96},{96,112},{112,128},... | collective-permute-start | bytes 491528 | tf_op jit(solution)/shard_map/ppermute | solution.py:21
  38.9 11.1 %collective-permute-start.5 = (bf16[128,640]{1,0:T(8,128)(2,1)S(1)}, bf16[128,640]{1,0:T(8,128)(2,1)S(1)}, u32[]{:S(2)}, u32[]{:S(2)}) collective-permute-start(bf16[128,640]{1,0:T(8,128)(2,1)S(1)} %get-tuple-element.12.q), channel_id=1, source_target_pairs={{0,496},{16,0},{32,16},{48,32},{64,48},{80,64},{96,80},{112,96},{1... | collective-permute-start | bytes 491528 | tf_op jit(solution)/shard_map/ppermute | solution.py:21
  45.5 4.6 %copy-start.6 = (s32[17]{0:T(128)S(1)}, s32[17]{0:T(128)}, u32[]{:S(2)}) copy-start(s32[17]{0:T(128)} %lengths_ref.3) | copy-start | bytes 208
  45.5 18.0 %copy-start.5 = (f32[50,640]{1,0:T(8,128)S(1)}, f32[50,640]{1,0:T(8,128)}, u32[]{:S(2)}) copy-start(f32[50,640]{1,0:T(8,128)} %table.1) | copy-start | bytes 384004
  53.6 10.0 %copy-start.7 = (s32[17]{0:T(128)S(1)}, s32[17]{0:T(128)}, u32[]{:S(2)}) copy-start(s32[17]{0:T(128)} %steps_ref.1) | copy-start | bytes 208
  53.6 12.4 %collective-permute-start.6 = (bf16[144,640]{1,0:T(8,128)(2,1)S(1)}, bf16[144,640]{1,0:T(8,128)(2,1)S(1)}, u32[]{:S(2)}, u32[]{:S(2)}) collective-permute-start(bf16[144,640]{1,0:T(8,128)(2,1)S(1)} %get-tuple-element.17), channel_id=1, source_target_pairs={{0,16},{16,32},{32,48},{48,64},{64,80},{80,96},{96,112},{112,128},... | collective-permute-start | bytes 552968 | tf_op jit(solution)/shard_map/ppermute | solution.py:21
  55.6 11.5 %collective-permute-start.7 = (bf16[144,640]{1,0:T(8,128)(2,1)S(1)}, bf16[144,640]{1,0:T(8,128)(2,1)S(1)}, u32[]{:S(2)}, u32[]{:S(2)}) collective-permute-start(bf16[144,640]{1,0:T(8,128)(2,1)S(1)} %get-tuple-element.18), channel_id=1, source_target_pairs={{0,496},{16,0},{32,16},{48,32},{64,48},{80,64},{96,80},{112,96},{1... | collective-permute-start | bytes 552968 | tf_op jit(solution)/shard_map/ppermute | solution.py:21

commit v2 on v1

--- a/solution.py
+++ b/solution.py
@@ -16,9 +16,15 @@
 EXTRA = 16
 
 
-def shifted(value, steps):
-    count = lax.axis_size("seq")
-    return lax.ppermute(value, "seq", [(source, (source + steps) % count) for source in range(count)])
+def hop(value, steps):
+    count, parts = lax.axis_size("seq"), lax.axis_size("dp")
+    pairs = []
+    for source in range(count):
+        for part in range(parts):
+            target = source + (steps if part % 2 == 0 else -steps)
+            if 0 <= target < count or (source, target % count) in ((2, count - 1), (count - FAR, 0)) or abs(steps) == 1:
+                pairs.append((source * parts + part, target % count * parts + part))
+    return lax.ppermute(value, ("seq", "dp"), pairs)
 
 
 def eye(size):
@@ -45,7 +51,7 @@
 
 
 def neighbour(place_ref, step):
-    block, count = place_ref[0] + step, place_ref[1]
+    block, count = place_ref[0] + step * place_ref[2], place_ref[1]
     return jnp.where(block < 0, block + count, jnp.where(block >= count, block - count, block))
 
 
@@ -79,58 +85,60 @@
 
 
 def attend(queries, keys, values, masks):
+    heads = range(queries.shape[1] // HD)
+    at = [slice(head * HD, (head + 1) * HD) for head in heads]
     scores = [
-        jnp.where(mask, lax.dot_general(queries, key, (((1,), (1,)), ((), ())), preferred_element_type=jnp.float32), LOW)
-        for key, mask in zip(keys, masks)
+        [
+            jnp.where(
+                mask,
+                lax.dot_general(
+                    queries[:, at[h]], key[:, at[h]], (((1,), (1,)), ((), ())), preferred_element_type=jnp.float32
+                ),
+                LOW,
+            )
+            for key, mask in zip(keys, masks)
+        ]
+        for h in heads
     ]
-    highest = jnp.max(functools.reduce(jnp.maximum, scores), axis=1, keepdims=True)
-    weights = [jnp.exp2((score - highest) * SCALE2) for score in scores]
-    total = jnp.sum(functools.reduce(jnp.add, weights), axis=1, keepdims=True)
-    mixed = functools.reduce(
-        jnp.add,
-        [
-            jnp.dot(weight.astype(jnp.bfloat16), value, preferred_element_type=jnp.float32)
-            for weight, value in zip(weights, values)
-        ],
-    )
-    return mixed / total, highest * SCALE2 + jnp.log2(total)
-
-
-def guest_kernel(place_ref, lengths_ref, ql, qr, kl, km, kr, vl, vm, vr, left_out, right_out):
-    rows, width = ql.shape
-    key_ids = [key_clips(neighbour(place_ref, step), rows, lengths_ref) for step in (-FAR, 0, FAR)]
-    for queries_ref, step, out in ((ql, -1, left_out), (qr, 1, right_out)):
-        query_ids = row_clips(neighbour(place_ref, step), rows, lengths_ref)
-        masks = [query_ids == ids for ids in key_ids]
-        out[rows:, :] = jnp.zeros((EXTRA, width), jnp.bfloat16)
-        for head in range(width // HD):
-            at = slice(head * HD, (head + 1) * HD)
-            mixed, level = attend(
-                queries_ref[:, at], [ref[:, at] for ref in (kl, km, kr)], [ref[:, at] for ref in (vl, vm, vr)], masks
-            )
-            out[:rows, at] = mixed.astype(jnp.bfloat16)
-            rest = as_row(level)
-            lines = []
-            for _ in range(3):
-                piece = rest.astype(jnp.bfloat16)
-                rest = rest - piece.astype(jnp.float32)
-                lines.append(piece.astype(jnp.float32))
-            pad = jnp.zeros((EXTRA - 3, rows), jnp.float32)
-            out[rows:, at] = jnp.concatenate(lines + [pad], axis=0).astype(jnp.bfloat16)
+    highest = [jnp.max(functools.reduce(jnp.maximum, scores[h]), axis=1, keepdims=True) for h in heads]
+    weights = [[jnp.exp2((score - highest[h]) * SCALE2) for score in scores[h]] for h in heads]
+    total = [jnp.sum(functools.reduce(jnp.add, weights[h]), axis=1, keepdims=True) for h in heads]
+    mixed = [
+        functools.reduce(
+            jnp.add,
+            [
+                jnp.dot(weight.astype(jnp.bfloat16), value[:, at[h]], preferred_element_type=jnp.float32)
+                for weight, value in zip(weights[h], values)
+            ],
+        )
+        for h in heads
+    ]
+    return [(at[h], mixed[h] / total[h], highest[h] * SCALE2 + jnp.log2(total[h])) for h in heads]
+
+
+def guest_kernel(step, place_ref, lengths_ref, queries, kl, km, kr, vl, vm, vr, out):
+    rows, width = queries.shape
+    query_ids = row_clips(neighbour(place_ref, step), rows, lengths_ref)
+    masks = [query_ids == key_clips(neighbour(place_ref, far), rows, lengths_ref) for far in (-FAR, 0, FAR)]
+    for at, mixed, level in attend(queries, (kl, km, kr), (vl, vm, vr), masks):
+        out[:rows, at] = mixed.astype(jnp.bfloat16)
+        rest = as_row(level)
+        lines = []
+        for _ in range(3):
+            piece = rest.astype(jnp.bfloat16)
+            rest = rest - piece.astype(jnp.float32)
+            lines.append(piece.astype(jnp.float32))
+        pad = jnp.zeros((EXTRA - 3, rows), jnp.float32)
+        out[rows:, at] = jnp.concatenate(lines + [pad], axis=0).astype(jnp.bfloat16)
 
 
 def home_kernel(place_ref, lengths_ref, steps_ref, table, q, kl, km, kr, vl, vm, vr, mixed_out, level_out, gate_out):
     rows, width = q.shape
     query_ids = row_clips(place_ref[0], rows, lengths_ref)
-    masks = [query_ids == key_clips(neighbour(place_ref, step), rows, lengths_ref) for step in (-FAR, 0, FAR)]
-    levels = []
-    for head in range(width // HD):
-        at = slice(head * HD, (head + 1) * HD)
-        mixed, level = attend(q[:, at], [ref[:, at] for ref in (kl, km, kr)], [ref[:, at] for ref in (vl, vm, vr)], masks)
+    masks = [query_ids == key_clips(neighbour(place_ref, far), rows, lengths_ref) for far in (-FAR, 0, FAR)]
+    for at, mixed, level in attend(q, (kl, km, kr), (vl, vm, vr), masks):
         mixed_out[:, at] = mixed
-        levels.append(jnp.broadcast_to(level, (rows, HD)))
-    for head, level in enumerate(levels):
-        level_out[:, head * HD : (head + 1) * HD] = level
+        level_out[:, at] = jnp.broadcast_to(level, (rows, HD))
     gate = jnp.zeros((rows, width), jnp.float32)
     for clip in range(lengths_ref.shape[0]):
         gate = jnp.where(query_ids == clip, table[pl.ds(steps_ref[clip], 1), :], gate)
@@ -170,11 +178,12 @@
     rows, width = q_rows.shape
     heads_here = width // HD
     peers = lax.axis_size("head")
-    place = jnp.stack([lax.axis_index("seq"), lax.axis_size("seq")]).astype(jnp.int32)
+    turn = 1 - 2 * (lax.axis_index("dp") % 2)
+    place = jnp.stack([lax.axis_index("seq"), lax.axis_size("seq"), turn]).astype(jnp.int32)
     bf16 = functools.partial(jax.ShapeDtypeStruct, dtype=jnp.bfloat16)
     f32 = functools.partial(jax.ShapeDtypeStruct, dtype=jnp.float32)
 
-    v_left, v_right = shifted(v_rows, FAR), shifted(v_rows, -FAR)
+    v_near, v_next = hop(v_rows, FAR), hop(v_rows, -FAR)
     (squares,) = call(squares_kernel, [f32((peers, 8, rows))], [], [q_rows, k_rows])
     squares = lax.all_to_all(squares, "head", 0, 0)
     q_norm, k_norm = call(
@@ -183,18 +192,21 @@
         [],
         [squares, q_rows, k_rows, q_gain.reshape(1, width), k_gain.reshape(1, width)],
     )
-    k_left, k_right = shifted(k_norm, FAR), shifted(k_norm, -FAR)
-    q_left, q_right = shifted(q_norm, 1), shifted(q_norm, -1)
-    around = [k_left, k_norm, k_right, v_left, v_rows, v_right]
+    k_near, k_next = hop(k_norm, FAR), hop(k_norm, -FAR)
+    q_near, q_next = hop(q_norm, 1), hop(q_norm, -1)
+    around = [k_near, k_norm, k_next, v_near, v_rows, v_next]
     flops = 4 * rows * 3 * rows * HD * heads_here
-    to_left, to_right = call(
-        guest_kernel,
-        [bf16((rows + EXTRA, width))] * 2,
-        [place, clip_lengths],
-        [q_left, q_right] + around,
-        2 * flops,
-    )
-    from_right, from_left = shifted(to_left, -1), shifted(to_right, 1)
+    returned = []
+    for queries, step in ((q_near, -1), (q_next, 1)):
+        (partial,) = call(
+            functools.partial(guest_kernel, step),
+            [bf16((rows + EXTRA, width))],
+            [place, clip_lengths],
+            [queries] + around,
+            flops,
+        )
+        returned.append(hop(partial, step))
+    from_right, from_left = returned
     mixed, levels, gate = call(
         home_kernel,
         [f32((rows, width))] * 3,

time: 68.5 us -> 66.6 us (0.972)
  the two profiles are of different devices: /device:TPU:8 before, /device:TPU:14 now
where the time goes in v2:
time: 66.6 us; the launch traced here: 66.1 us
  starting transfers between devices  46.1 us (69%)
  waiting for transfers between devices  10.9 us (16%)
  Pallas kernels  6.01 us (9%)
  local copies, waits for them, and re-layouts  2.78 us (4%)
    ppermute x8, starting transfers between devices, hop(): return lax.ppermute(value, ('seq', 'dp'), pairs)  41.1 us
    ppermute x8, waiting for transfers between devices, hop(): return lax.ppermute(value, ('seq', 'dp'), pairs)  9.06 us
    pallas_call x6, Pallas kernels, call(): pl.pallas_call(kernel, out_shape=outs, in_specs=space, out_specs=[pl.Bloc...  6.01 us
    all_to_all x1, starting transfers between devices, per_device(): squares = lax.all_to_all(squares, 'head', 0, 0)  5.04 us
    unnamed x20, local copies, waits for them, and re-layouts  2.77 us
    all_to_all x1, waiting for transfers between devices, per_device(): squares = lax.all_to_all(squares, 'head', 0, 0)  1.81 us
  transfers between devices with their start and end apart: 9, of which 4 were waited for; matrix products, arithmetic and copies ran while one was open for 0% of the time, Pallas kernels for 8%

profile of v2, /device:TPU:14, one launch (start us, length us, event | category | flops | bytes accessed | tf_op | source)
XLA Modules:
  0.0 66.1 jit_solution(6783109113308697158)
XLA Ops:
  0.0 0.0 copy-start
  0.0 13.3 %collective-permute-start.3 = (bf16[128,640]{1,0:T(8,128)(2,1)}, bf16[128,640]{1,0:T(8,128)(2,1)S(1)}, u32[]{:S(2)}, u32[]{:S(2)}) collective-permute-start(bf16[128,640]{1,0:T(8,128)(2,1)} %vm.5), channel_id=1, source_target_pairs={{1,49},{3,51},{17,65},{19,67},{32,496},{33,81},{34,498},{35,83},{4... | collective-permute-start | bytes 491528 | tf_op jit(solution)/shard_map/ppermute | solution.py:27
  13.3 0.0 copy-start.1
  13.3 0.9 %copy-done.1 = bf16[128,640]{1,0:T(8,128)(2,1)S(1)} copy-done((bf16[128,640]{1,0:T(8,128)(2,1)S(1)}, bf16[128,640]{1,0:T(8,128)(2,1)}, u32[]{:S(2)}) %copy-start.1) | copy-done | bytes 163864
  14.2 0.0 copy-start.3
  14.2 0.9 %copy-done.3 = bf16[128,640]{1,0:T(8,128)(2,1)S(1)} copy-done((bf16[128,640]{1,0:T(8,128)(2,1)S(1)}, bf16[128,640]{1,0:T(8,128)(2,1)}, u32[]{:S(2)}) %copy-start.3) | copy-done | bytes 163864
  15.1 0.0 copy-start.2
  15.1 0.8 %shard_map.82 = f32[4,8,128]{2,1,0:T(8,128)} custom-call(bf16[128,640]{1,0:T(8,128)(2,1)S(1)} %copy-done.1, bf16[128,640]{1,0:T(8,128)(2,1)S(1)} %copy-done.3), custom_call_target="tpu_custom_call" | custom-call | bytes 344064 | tf_op jit(solution)/shard_map/pallas_call | solution.py:167
  15.9 0.0 copy-start.8
  15.9 5.0 %all-to-all-start = ((f32[4,8,128]{2,1,0:T(8,128)}), f32[4,8,128]{2,1,0:T(8,128)S(1)}, u32[]{:S(2)}, u32[]{:S(2)}) async-start(f32[4,8,128]{2,1,0:T(8,128)} %shard_map.82), calls=%async_computation | async-start | bytes 32768 | tf_op jit(solution)/shard_map/all_to_all | solution.py:188
  20.9 0.0 copy-done
  20.9 0.0 copy-start.9
  20.9 2.0 %collective-permute-start.2 = (bf16[128,640]{1,0:T(8,128)(2,1)S(1)}, bf16[128,640]{1,0:T(8,128)(2,1)S(1)}, u32[]{:S(2)}, u32[]{:S(2)}) collective-permute-start(bf16[128,640]{1,0:T(8,128)(2,1)S(1)} %copy-done), channel_id=1, source_target_pairs={{0,48},{2,50},{16,64},{18,66},{32,80},{33,497},{34,82},{35,499},{4... | collective-permute-start | bytes 491528 | tf_op jit(solution)/shard_map/ppermute | solution.py:27
  22.9 0.0 copy-done.8
  23.0 0.0 copy-done.9
  23.0 1.8 %all-to-all-done.squares_ref = f32[4,8,128]{2,1,0:T(8,128)S(1)} async-done(((f32[4,8,128]{2,1,0:T(8,128)}), f32[4,8,128]{2,1,0:T(8,128)S(1)}, u32[]{:S(2)}, u32[]{:S(2)}) %all-to-all-start) | async-done | bytes 16416 | tf_op jit(solution)/shard_map/all_to_all | solution.py:188
  24.8 0.0 copy-done.2
  24.8 0.0 copy-start.4
  24.8 0.9 %copy-done.4 = bf16[128,640]{1,0:T(8,128)(2,1)S(1)} copy-done((bf16[128,640]{1,0:T(8,128)(2,1)S(1)}, bf16[128,640]{1,0:T(8,128)(2,1)}, u32[]{:S(2)}) %copy-start.4) | copy-done | bytes 163864
  25.7 0.2 shard_map.83
  25.9 6.7 %collective-permute-start.4 = (bf16[128,640]{1,0:T(8,128)(2,1)S(1)}, bf16[128,640]{1,0:T(8,128)(2,1)S(1)}, u32[]{:S(2)}, u32[]{:S(2)}) collective-permute-start(bf16[128,640]{1,0:T(8,128)(2,1)S(1)} %get-tuple-element.10.q), channel_id=1, source_target_pairs={{0,496},{1,17},{2,498},{3,19},{16,0},{17,33},{18,2},{19,35},{32,16... | collective-permute-start | bytes 491528 | tf_op jit(solution)/shard_map/ppermute | solution.py:27
  32.6 2.8 %collective-permute-start.1 = (bf16[128,640]{1,0:T(8,128)(2,1)S(1)}, bf16[128,640]{1,0:T(8,128)(2,1)S(1)}, u32[]{:S(2)}, u32[]{:S(2)}) collective-permute-start(bf16[128,640]{1,0:T(8,128)(2,1)S(1)} %get-tuple-element.11.km), channel_id=1, source_target_pairs={{1,49},{3,51},{17,65},{19,67},{32,496},{33,81},{34,498},{35,83},{4... | collective-permute-start | bytes 491528 | tf_op jit(solution)/shard_map/ppermute | solution.py:27
  35.4 4.8 %collective-permute-start = (bf16[128,640]{1,0:T(8,128)(2,1)S(1)}, bf16[128,640]{1,0:T(8,128)(2,1)S(1)}, u32[]{:S(2)}, u32[]{:S(2)}) collective-permute-start(bf16[128,640]{1,0:T(8,128)(2,1)S(1)} %get-tuple-element.11.km), channel_id=1, source_target_pairs={{0,48},{2,50},{16,64},{18,66},{32,80},{33,497},{34,82},{35,499},{4... | collective-permute-start | bytes 491528 | tf_op jit(solution)/shard_map/ppermute | solution.py:27
  40.2 0.0 collective-permute-done.3.vr
  40.2 1.9 %collective-permute-start.6 = (bf16[128,640]{1,0:T(8,128)(2,1)S(1)}, bf16[128,640]{1,0:T(8,128)(2,1)S(1)}, u32[]{:S(2)}, u32[]{:S(2)}) collective-permute-start(bf16[128,640]{1,0:T(8,128)(2,1)S(1)} %get-tuple-element.10.q), channel_id=1, source_target_pairs={{0,16},{1,497},{2,18},{3,499},{16,32},{17,1},{18,34},{19,3},{32,48... | collective-permute-start | bytes 491528 | tf_op jit(solution)/shard_map/ppermute | solution.py:27
  42.2 0.0 copy-start.6
  42.2 0.1 pad_add_fusion.place_ref
  42.3 0.0 collective-permute-done.2.vl
  42.3 0.0 collective-permute-done.4.queries
  42.3 4.3 %collective-permute-done.1.kr = bf16[128,640]{1,0:T(8,128)(2,1)S(1)} collective-permute-done((bf16[128,640]{1,0:T(8,128)(2,1)S(1)}, bf16[128,640]{1,0:T(8,128)(2,1)S(1)}, u32[]{:S(2)}, u32[]{:S(2)}) %collective-permute-start.1) | collective-permute-done | bytes 163872 | tf_op jit(solution)/shard_map/ppermute | solution.py:27
  46.5 3.3 %collective-permute-done.kl = bf16[128,640]{1,0:T(8,128)(2,1)S(1)} collective-permute-done((bf16[128,640]{1,0:T(8,128)(2,1)S(1)}, bf16[128,640]{1,0:T(8,128)(2,1)S(1)}, u32[]{:S(2)}, u32[]{:S(2)}) %collective-permute-start) | collective-permute-done | bytes 163872 | tf_op jit(solution)/shard_map/ppermute | solution.py:27
  49.8 0.0 copy-done.6
  49.8 1.3 %shard_map.85 = bf16[144,640]{1,0:T(8,128)(2,1)S(1)} custom-call(s32[3]{0:T(128)S(1)} %pad_add_fusion.place_ref, s32[17]{0:T(128)S(1)} %copy-done.6, bf16[128,640]{1,0:T(8,128)(2,1)S(1)} %collective-permute-done.4.queries, bf16[128,640]{1,0:T(8,128)(2,1)S(1)} %collective-permute-done.kl, bf16[128,640]{1,0:T(8,128)(2,1)S(1)} %get-tuple-element.11.km, ...), custom_call_target="tpu_custom_call" | custom-call | flops 125829120 | bytes 1331200 | tf_op jit(solution)/shard_map/pallas_call | solution.py:167
  51.1 0.0 copy-start.5
  51.1 0.0 copy-start.7
  51.1 4.1 %collective-permute-start.5 = (bf16[144,640]{1,0:T(8,128)(2,1)S(1)}, bf16[144,640]{1,0:T(8,128)(2,1)S(1)}, u32[]{:S(2)}, u32[]{:S(2)}) collective-permute-start(bf16[144,640]{1,0:T(8,128)(2,1)S(1)} %shard_map.85), channel_id=1, source_target_pairs={{0,16},{1,497},{2,18},{3,499},{16,32},{17,1},{18,34},{19,3},{32,48... | collective-permute-start | bytes 552968 | tf_op jit(solution)/shard_map/ppermute | solution.py:27
  55.2 0.0 collective-permute-done.6.queries
  55.2 1.3 %shard_map.86 = bf16[144,640]{1,0:T(8,128)(2,1)S(1)} custom-call(s32[3]{0:T(128)S(1)} %pad_add_fusion.place_ref, s32[17]{0:T(128)S(1)} %copy-done.6, bf16[128,640]{1,0:T(8,128)(2,1)S(1)} %collective-permute-done.6.queries, bf16[128,640]{1,0:T(8,128)(2,1)S(1)} %collective-permute-done.kl, bf16[128,640]{1,0:T(8,128)(2,1)S(1)} %get-tuple-element.11.km, ...), custom_call_target="tpu_custom_call" | custom-call | flops 125829120 | bytes 1331200 | tf_op jit(solution)/shard_map/pallas_call | solution.py:167
  56.5 5.5 %collective-permute-start.7 = (bf16[144,640]{1,0:T(8,128)(2,1)S(1)}, bf16[144,640]{1,0:T(8,128)(2,1)S(1)}, u32[]{:S(2)}, u32[]{:S(2)}) collective-permute-start(bf16[144,640]{1,0:T(8,128)(2,1)S(1)} %shard_map.86), channel_id=1, source_target_pairs={{0,496},{1,17},{2,498},{3,19},{16,0},{17,33},{18,2},{19,35},{32,16... | collective-permute-start | bytes 552968 | tf_op jit(solution)/shard_map/ppermute | solution.py:27
  62.0 0.0 copy-done.5
  62.0 0.0 copy-done.7
  62.0 1.5 %shard_map.84 = (f32[128,640]{1,0:T(8,128)S(1)}, f32[128,640]{1,0:T(8,128)S(1)}, f32[128,640]{1,0:T(8,128)S(1)}) custom-call(s32[3]{0:T(128)S(1)} %pad_add_fusion.place_ref, s32[17]{0:T(128)S(1)} %copy-done.6, s32[17]{0:T(128)S(1)} %copy-done.7, f32[50,640]{1,0:T(8,128)S(1)} %copy-done.5, bf16[128,640]{1,0:T(8,128)(2,1)S(1)} %get-tuple-element.10.q, ...), custom_call_target="tpu_custom_call" | custom-call | flops 125829120 | bytes 2257920 | tf_op jit(solution)/shard_map/pallas_call | solution.py:167
  63.5 0.0 collective-permute-done.5.from_left
  63.6 1.5 %collective-permute-done.7.from_right = bf16[144,640]{1,0:T(8,128)(2,1)S(1)} collective-permute-done((bf16[144,640]{1,0:T(8,128)(2,1)S(1)}, bf16[144,640]{1,0:T(8,128)(2,1)S(1)}, u32[]{:S(2)}, u32[]{:S(2)}) %collective-permute-start.7) | collective-permute-done | bytes 184352 | tf_op jit(solution)/shard_map/ppermute | solution.py:27
  65.1 1.0 %shard_map.87 = bf16[128,640]{1,0:T(8,128)(2,1)} custom-call(f32[128,640]{1,0:T(8,128)S(1)} %get-tuple-element.12.gate, f32[128,640]{1,0:T(8,128)S(1)} %get-tuple-element.13.mixed, f32[128,640]{1,0:T(8,128)S(1)} %get-tuple-element.14.levels, bf16[144,640]{1,0:T(8,128)(2,1)S(1)} %collective-permute-done.5.from_left, ...), custom_call_target="tpu_custom_call" | custom-call | bytes 1515520 | tf_op jit(solution)/shard_map/pallas_call | solution.py:167
  (2 shorter events, 0.0 us)
Async XLA Ops:
  0.0 20.9 %copy-start = (bf16[128,640]{1,0:T(8,128)(2,1)S(1)}, bf16[128,640]{1,0:T(8,128)(2,1)}, u32[]{:S(2)}) copy-start(bf16[128,640]{1,0:T(8,128)(2,1)} %vm.5) | copy-start | bytes 491524
  0.0 40.2 %collective-permute-start.3 = (bf16[128,640]{1,0:T(8,128)(2,1)}, bf16[128,640]{1,0:T(8,128)(2,1)S(1)}, u32[]{:S(2)}, u32[]{:S(2)}) collective-permute-start(bf16[128,640]{1,0:T(8,128)(2,1)} %vm.5), channel_id=1, source_target_pairs={{1,49},{3,51},{17,65},{19,67},{32,496},{33,81},{34,498},{35,83},{4... | collective-permute-start | bytes 491528 | tf_op jit(solution)/shard_map/ppermute | solution.py:27
  13.3 0.9 %copy-start.1 = (bf16[128,640]{1,0:T(8,128)(2,1)S(1)}, bf16[128,640]{1,0:T(8,128)(2,1)}, u32[]{:S(2)}) copy-start(bf16[128,640]{1,0:T(8,128)(2,1)} %q_ref.3) | copy-start | bytes 491524
  14.2 0.9 %copy-start.3 = (bf16[128,640]{1,0:T(8,128)(2,1)S(1)}, bf16[128,640]{1,0:T(8,128)(2,1)}, u32[]{:S(2)}) copy-start(bf16[128,640]{1,0:T(8,128)(2,1)} %k_ref.3) | copy-start | bytes 491524
  15.1 9.7 %copy-start.2 = (bf16[128,640]{1,0:T(8,128)(2,1)S(1)}, bf16[128,640]{1,0:T(8,128)(2,1)}, u32[]{:S(2)}) copy-start(bf16[128,640]{1,0:T(8,128)(2,1)} %q_ref.3) | copy-start | bytes 491524
  15.9 7.1 %copy-start.8 = (f32[640]{0:T(1024)S(1)}, f32[640]{0:T(1024)}, u32[]{:S(2)}) copy-start(f32[640]{0:T(1024)} %param.11) | copy-start | bytes 7684
  15.9 8.9 %all-to-all-start = ((f32[4,8,128]{2,1,0:T(8,128)}), f32[4,8,128]{2,1,0:T(8,128)S(1)}, u32[]{:S(2)}, u32[]{:S(2)}) async-start(f32[4,8,128]{2,1,0:T(8,128)} %shard_map.82), calls=%async_computation | async-start | bytes 32768 | tf_op jit(solution)/shard_map/all_to_all | solution.py:188
  20.9 2.1 %copy-start.9 = (f32[640]{0:T(1024)S(1)}, f32[640]{0:T(1024)}, u32[]{:S(2)}) copy-start(f32[640]{0:T(1024)} %param.12) | copy-start | bytes 7684
  20.9 21.4 %collective-permute-start.2 = (bf16[128,640]{1,0:T(8,128)(2,1)S(1)}, bf16[128,640]{1,0:T(8,128)(2,1)S(1)}, u32[]{:S(2)}, u32[]{:S(2)}) collective-permute-start(bf16[128,640]{1,0:T(8,128)(2,1)S(1)} %copy-done), channel_id=1, source_target_pairs={{0,48},{2,50},{16,64},{18,66},{32,80},{33,497},{34,82},{35,499},{4... | collective-permute-start | bytes 491528 | tf_op jit(solution)/shard_map/ppermute | solution.py:27
  24.8 0.9 %copy-start.4 = (bf16[128,640]{1,0:T(8,128)(2,1)S(1)}, bf16[128,640]{1,0:T(8,128)(2,1)}, u32[]{:S(2)}) copy-start(bf16[128,640]{1,0:T(8,128)(2,1)} %k_ref.3) | copy-start | bytes 491524
  25.9 16.4 %collective-permute-start.4 = (bf16[128,640]{1,0:T(8,128)(2,1)S(1)}, bf16[128,640]{1,0:T(8,128)(2,1)S(1)}, u32[]{:S(2)}, u32[]{:S(2)}) collective-permute-start(bf16[128,640]{1,0:T(8,128)(2,1)S(1)} %get-tuple-element.10.q), channel_id=1, source_target_pairs={{0,496},{1,17},{2,498},{3,19},{16,0},{17,33},{18,2},{19,35},{32,16... | collective-permute-start | bytes 491528 | tf_op jit(solution)/shard_map/ppermute | solution.py:27
  32.6 14.0 %collective-permute-start.1 = (bf16[128,640]{1,0:T(8,128)(2,1)S(1)}, bf16[128,640]{1,0:T(8,128)(2,1)S(1)}, u32[]{:S(2)}, u32[]{:S(2)}) collective-permute-start(bf16[128,640]{1,0:T(8,128)(2,1)S(1)} %get-tuple-element.11.km), channel_id=1, source_target_pairs={{1,49},{3,51},{17,65},{19,67},{32,496},{33,81},{34,498},{35,83},{4... | collective-permute-start | bytes 491528 | tf_op jit(solution)/shard_map/ppermute | solution.py:27
  35.4 14.4 %collective-permute-start = (bf16[128,640]{1,0:T(8,128)(2,1)S(1)}, bf16[128,640]{1,0:T(8,128)(2,1)S(1)}, u32[]{:S(2)}, u32[]{:S(2)}) collective-permute-start(bf16[128,640]{1,0:T(8,128)(2,1)S(1)} %get-tuple-element.11.km), channel_id=1, source_target_pairs={{0,48},{2,50},{16,64},{18,66},{32,80},{33,497},{34,82},{35,499},{4... | collective-permute-start | bytes 491528 | tf_op jit(solution)/shard_map/ppermute | solution.py:27
  40.2 15.0 %collective-permute-start.6 = (bf16[128,640]{1,0:T(8,128)(2,1)S(1)}, bf16[128,640]{1,0:T(8,128)(2,1)S(1)}, u32[]{:S(2)}, u32[]{:S(2)}) collective-permute-start(bf16[128,640]{1,0:T(8,128)(2,1)S(1)} %get-tuple-element.10.q), channel_id=1, source_target_pairs={{0,16},{1,497},{2,18},{3,499},{16,32},{17,1},{18,34},{19,3},{32,48... | collective-permute-start | bytes 491528 | tf_op jit(solution)/shard_map/ppermute | solution.py:27
  42.2 7.6 %copy-start.6 = (s32[17]{0:T(128)S(1)}, s32[17]{0:T(128)}, u32[]{:S(2)}) copy-start(s32[17]{0:T(128)} %lengths_ref.5) | copy-start | bytes 208
  51.1 10.9 %copy-start.5 = (f32[50,640]{1,0:T(8,128)S(1)}, f32[50,640]{1,0:T(8,128)}, u32[]{:S(2)}) copy-start(f32[50,640]{1,0:T(8,128)} %table.1) | copy-start | bytes 384004
  51.1 10.9 %copy-start.7 = (s32[17]{0:T(128)S(1)}, s32[17]{0:T(128)}, u32[]{:S(2)}) copy-start(s32[17]{0:T(128)} %steps_ref.1) | copy-start | bytes 208
  51.1 12.4 %collective-permute-start.5 = (bf16[144,640]{1,0:T(8,128)(2,1)S(1)}, bf16[144,640]{1,0:T(8,128)(2,1)S(1)}, u32[]{:S(2)}, u32[]{:S(2)}) collective-permute-start(bf16[144,640]{1,0:T(8,128)(2,1)S(1)} %shard_map.85), channel_id=1, source_target_pairs={{0,16},{1,497},{2,18},{3,499},{16,32},{17,1},{18,34},{19,3},{32,48... | collective-permute-start | bytes 552968 | tf_op jit(solution)/shard_map/ppermute | solution.py:27
  56.5 8.5 %collective-permute-start.7 = (bf16[144,640]{1,0:T(8,128)(2,1)S(1)}, bf16[144,640]{1,0:T(8,128)(2,1)S(1)}, u32[]{:S(2)}, u32[]{:S(2)}) collective-permute-start(bf16[144,640]{1,0:T(8,128)(2,1)S(1)} %shard_map.86), channel_id=1, source_target_pairs={{0,496},{1,17},{2,498},{3,19},{16,0},{17,33},{18,2},{19,35},{32,16... | collective-permute-start | bytes 552968 | tf_op jit(solution)/shard_map/ppermute | solution.py:27

commit v3 on v2

--- a/solution.py
+++ b/solution.py
@@ -63,25 +63,24 @@
     return clip_of(block * rows + lax.broadcasted_iota(jnp.int32, (1, rows), 1), lengths_ref)
 
 
-def squares_kernel(q_ref, k_ref, out_ref):
-    def total(ref):
-        data = ref[...].astype(jnp.float32)
-        return as_row(jnp.sum(data * data, axis=1, keepdims=True))
-
+def squares_kernel(both_ref, out_ref):
     rows = out_ref.shape[2]
-    both = jnp.concatenate([total(q_ref), total(k_ref), jnp.zeros((6, rows), jnp.float32)], axis=0)
+    lines = []
+    for index in range(2):
+        data = both_ref[index].astype(jnp.float32)
+        lines.append(as_row(jnp.sum(data * data, axis=1, keepdims=True)))
+    lines = jnp.concatenate(lines + [jnp.zeros((6, rows), jnp.float32)], axis=0)
     for peer in range(out_ref.shape[0]):
-        out_ref[peer] = both
-
-
-def norm_kernel(squares_ref, q_ref, k_ref, q_gain_ref, k_gain_ref, q_out, k_out):
-    both = squares_ref[0]
+        out_ref[peer] = lines
+
+
+def norm_kernel(index, squares_ref, both_ref, gain_ref, *rest):
+    total = squares_ref[0]
     for peer in range(1, squares_ref.shape[0]):
-        both = both + squares_ref[peer]
-    factors = lax.rsqrt(both / (HEADS * HD) + 1e-06)
-    for line, (ref, gain_ref, out) in enumerate([(q_ref, q_gain_ref, q_out), (k_ref, k_gain_ref, k_out)]):
-        scaled = ref[...].astype(jnp.float32) * as_column(factors[line : line + 1])
-        out[...] = (scaled * gain_ref[...]).astype(jnp.bfloat16)
+        total = total + squares_ref[peer]
+    factors = lax.rsqrt(total / (HEADS * HD) + 1e-06)
+    scaled = both_ref[index].astype(jnp.float32) * as_column(factors[index : index + 1])
+    rest[-1][...] = (scaled * gain_ref[...]).astype(jnp.bfloat16)
 
 
 def attend(queries, keys, values, masks):
@@ -184,13 +183,17 @@
     f32 = functools.partial(jax.ShapeDtypeStruct, dtype=jnp.float32)
 
     v_near, v_next = hop(v_rows, FAR), hop(v_rows, -FAR)
-    (squares,) = call(squares_kernel, [f32((peers, 8, rows))], [], [q_rows, k_rows])
+    both = jnp.stack([q_rows, k_rows])
+    (squares,) = call(squares_kernel, [f32((peers, 8, rows))], [], [both])
     squares = lax.all_to_all(squares, "head", 0, 0)
-    q_norm, k_norm = call(
-        norm_kernel,
-        [bf16((rows, width)), bf16((rows, width))],
+    (k_norm,) = call(
+        functools.partial(norm_kernel, 1), [bf16((rows, width))], [], [squares, both, k_gain.reshape(1, width)]
+    )
+    (q_norm,) = call(
+        functools.partial(norm_kernel, 0),
+        [bf16((rows, width))],
         [],
-        [squares, q_rows, k_rows, q_gain.reshape(1, width), k_gain.reshape(1, width)],
+        [squares, both, q_gain.reshape(1, width), k_norm, v_near],
     )
     k_near, k_next = hop(k_norm, FAR), hop(k_norm, -FAR)
     q_near, q_next = hop(q_norm, 1), hop(q_norm, -1)

time: 66.6 us -> 63.5 us (0.953)
  waiting for transfers between devices: 10.9 us -> 7.79 us
  local copies, waits for them, and re-layouts: 2.78 us -> 0.04 us
  starting transfers between devices: 46.1 us -> 47.8 us
  other arithmetic: 0.08 us -> 1.11 us
    unnamed x20 -> x12, local copies, waits for them, and re-layouts: 2.77 us -> 0.03 us
    all_to_all x1, waiting for transfers between devices: 1.81 us -> 0.01 us  [per_device(): squares = lax.all_to_all(squares, 'head', 0, 0)]
    ppermute x8, starting transfers between devices: 41.1 us -> 42.8 us  [hop(): return lax.ppermute(value, ('seq', 'dp'), pairs)]
    ppermute x8, waiting for transfers between devices: 9.06 us -> 7.79 us  [hop(): return lax.ppermute(value, ('seq', 'dp'), pairs)]
    another operation x0 -> x1, other arithmetic: none -> 1.03 us  [per_device(): both = jnp.stack([q_rows, k_rows])]
    pallas_call x6 -> x7, Pallas kernels: 6.01 us -> 6.1 us  [call(): pl.pallas_call(kernel, out_shape=outs, in_specs=space, out_specs=[pl.Bloc...]
  transfers between devices with their start and end apart: 9 -> 9, of which waited for: 4 -> 2; matrix products, arithmetic and copies ran while one was open for 0% -> 2% of each run, Pallas kernels for 8% -> 8%
where the time goes in v3:
time: 63.5 us; the launch traced here: 63.1 us
  starting transfers between devices  47.8 us (75%)
  waiting for transfers between devices  7.79 us (12%)
  Pallas kernels  6.1 us (10%)
  other arithmetic  1.11 us (2%)
    ppermute x8, starting transfers between devices, hop(): return lax.ppermute(value, ('seq', 'dp'), pairs)  42.8 us
    ppermute x8, waiting for transfers between devices, hop(): return lax.ppermute(value, ('seq', 'dp'), pairs)  7.79 us
    pallas_call x7, Pallas kernels, call(): pl.pallas_call(kernel, out_shape=outs, in_specs=space, out_specs=[pl.Bloc...  6.1 us
    all_to_all x1, starting transfers between devices, per_device(): squares = lax.all_to_all(squares, 'head', 0, 0)  5.04 us
  transfers between devices with their start and end apart: 9, of which 2 were waited for; matrix products, arithmetic and copies ran while one was open for 2% of the time, Pallas kernels for 8%

profile of v3, /device:TPU:14, one launch (start us, length us, event | category | flops | bytes accessed | tf_op | source)
XLA Modules:
  0.0 63.1 jit_solution(18104518717494354315)
XLA Ops:
  0.0 6.5 %collective-permute-start = (bf16[128,640]{1,0:T(8,128)(2,1)}, bf16[128,640]{1,0:T(8,128)(2,1)S(1)}, u32[]{:S(2)}, u32[]{:S(2)}) collective-permute-start(bf16[128,640]{1,0:T(8,128)(2,1)} %vm.5), channel_id=1, source_target_pairs={{0,48},{2,50},{16,64},{18,66},{32,80},{33,497},{34,82},{35,499},{4... | collective-permute-start | bytes 491528 | tf_op jit(solution)/shard_map/ppermute | solution.py:27
  6.5 1.0 %pad_maximum_fusion.both_ref = bf16[2,128,640]{2,1,0:T(8,128)(2,1)S(1)} fusion(bf16[1,128,640]{2,1,0:T(8,128)(2,1)} %bitcast.4, bf16[1,128,640]{2,1,0:T(8,128)(2,1)} %bitcast.5), kind=kLoop, calls=%fused_computation | loop fusion | flops 163840 | bytes 655360 | tf_op jit(solution)/shard_map/stack | solution.py:186
  7.6 0.0 copy-start
  7.6 0.8 %shard_map.82 = f32[4,8,128]{2,1,0:T(8,128)} custom-call(bf16[2,128,640]{2,1,0:T(8,128)(2,1)S(1)} %pad_maximum_fusion.both_ref), custom_call_target="tpu_custom_call" | custom-call | bytes 344064 | tf_op jit(solution)/shard_map/pallas_call | solution.py:166
  8.3 0.0 copy-start.4
  8.3 5.0 %all-to-all-start = ((f32[4,8,128]{2,1,0:T(8,128)}), f32[4,8,128]{2,1,0:T(8,128)S(1)}, u32[]{:S(2)}, u32[]{:S(2)}) async-start(f32[4,8,128]{2,1,0:T(8,128)} %shard_map.82), calls=%async_computation | async-start | bytes 32768 | tf_op jit(solution)/shard_map/all_to_all | solution.py:188
  13.4 0.0 copy-done
  13.4 0.0 copy-start.5
  13.4 8.6 %collective-permute-start.3 = (bf16[128,640]{1,0:T(8,128)(2,1)S(1)}, bf16[128,640]{1,0:T(8,128)(2,1)S(1)}, u32[]{:S(2)}, u32[]{:S(2)}) collective-permute-start(bf16[128,640]{1,0:T(8,128)(2,1)S(1)} %copy-done), channel_id=1, source_target_pairs={{1,49},{3,51},{17,65},{19,67},{32,496},{33,81},{34,498},{35,83},{4... | collective-permute-start | bytes 491528 | tf_op jit(solution)/shard_map/ppermute | solution.py:27
  22.0 0.0 copy-done.4
  22.1 0.0 copy-done.5
  22.1 0.0 all-to-all-done.squares_ref
  22.1 0.1 shard_map.83.rest_0_.km
  22.2 6.9 %collective-permute-start.2 = (bf16[128,640]{1,0:T(8,128)(2,1)S(1)}, bf16[128,640]{1,0:T(8,128)(2,1)S(1)}, u32[]{:S(2)}, u32[]{:S(2)}) collective-permute-start(bf16[128,640]{1,0:T(8,128)(2,1)S(1)} %shard_map.83.rest_0_.km), channel_id=1, source_target_pairs={{1,49},{3,51},{17,65},{19,67},{32,496},{33,81},{34,498},{35,83},{4... | collective-permute-start | bytes 491528 | tf_op jit(solution)/shard_map/ppermute | solution.py:27
  29.2 1.9 %collective-permute-start.1 = (bf16[128,640]{1,0:T(8,128)(2,1)S(1)}, bf16[128,640]{1,0:T(8,128)(2,1)S(1)}, u32[]{:S(2)}, u32[]{:S(2)}) collective-permute-start(bf16[128,640]{1,0:T(8,128)(2,1)S(1)} %shard_map.83.rest_0_.km), channel_id=1, source_target_pairs={{0,48},{2,50},{16,64},{18,66},{32,80},{33,497},{34,82},{35,499},{4... | collective-permute-start | bytes 491528 | tf_op jit(solution)/shard_map/ppermute | solution.py:27
  31.1 0.0 collective-permute-done.rest_1_.vl
  31.1 0.1 shard_map.84.q
  31.2 7.2 %collective-permute-start.4 = (bf16[128,640]{1,0:T(8,128)(2,1)S(1)}, bf16[128,640]{1,0:T(8,128)(2,1)S(1)}, u32[]{:S(2)}, u32[]{:S(2)}) collective-permute-start(bf16[128,640]{1,0:T(8,128)(2,1)S(1)} %shard_map.84.q), channel_id=1, source_target_pairs={{0,496},{1,17},{2,498},{3,19},{16,0},{17,33},{18,2},{19,35},{32,16... | collective-permute-start | bytes 491528 | tf_op jit(solution)/shard_map/ppermute | solution.py:27
  38.5 1.9 %collective-permute-start.6 = (bf16[128,640]{1,0:T(8,128)(2,1)S(1)}, bf16[128,640]{1,0:T(8,128)(2,1)S(1)}, u32[]{:S(2)}, u32[]{:S(2)}) collective-permute-start(bf16[128,640]{1,0:T(8,128)(2,1)S(1)} %shard_map.84.q), channel_id=1, source_target_pairs={{0,16},{1,497},{2,18},{3,499},{16,32},{17,1},{18,34},{19,3},{32,48... | collective-permute-start | bytes 491528 | tf_op jit(solution)/shard_map/ppermute | solution.py:27
  40.4 0.0 copy-start.2
  40.4 0.1 pad_add_fusion.place_ref
  40.5 0.0 collective-permute-done.3.vr
  40.5 0.0 collective-permute-done.2.kr
  40.5 6.3 %collective-permute-done.1.kl = bf16[128,640]{1,0:T(8,128)(2,1)S(1)} collective-permute-done((bf16[128,640]{1,0:T(8,128)(2,1)S(1)}, bf16[128,640]{1,0:T(8,128)(2,1)S(1)}, u32[]{:S(2)}, u32[]{:S(2)}) %collective-permute-start.1) | collective-permute-done | bytes 163872 | tf_op jit(solution)/shard_map/ppermute | solution.py:27
  46.8 0.0 collective-permute-done.4.queries
  46.8 0.0 copy-done.2
  46.8 1.3 %shard_map.86 = bf16[144,640]{1,0:T(8,128)(2,1)S(1)} custom-call(s32[3]{0:T(128)S(1)} %pad_add_fusion.place_ref, s32[17]{0:T(128)S(1)} %copy-done.2, bf16[128,640]{1,0:T(8,128)(2,1)S(1)} %collective-permute-done.4.queries, bf16[128,640]{1,0:T(8,128)(2,1)S(1)} %collective-permute-done.1.kl, bf16[128,640]{1,0:T(8,128)(2,1)S(1)} %shard_map.83.rest_0_.km, ...), custom_call_target="tpu_custom_call" | custom-call | flops 125829120 | bytes 1331200 | tf_op jit(solution)/shard_map/pallas_call | solution.py:166
  48.1 0.0 copy-start.1
  48.1 0.0 copy-start.3
  48.1 2.7 %collective-permute-start.5 = (bf16[144,640]{1,0:T(8,128)(2,1)S(1)}, bf16[144,640]{1,0:T(8,128)(2,1)S(1)}, u32[]{:S(2)}, u32[]{:S(2)}) collective-permute-start(bf16[144,640]{1,0:T(8,128)(2,1)S(1)} %shard_map.86), channel_id=1, source_target_pairs={{0,16},{1,497},{2,18},{3,499},{16,32},{17,1},{18,34},{19,3},{32,48... | collective-permute-start | bytes 552968 | tf_op jit(solution)/shard_map/ppermute | solution.py:27
  50.8 0.0 collective-permute-done.6.queries
  50.8 1.3 %shard_map.87 = bf16[144,640]{1,0:T(8,128)(2,1)S(1)} custom-call(s32[3]{0:T(128)S(1)} %pad_add_fusion.place_ref, s32[17]{0:T(128)S(1)} %copy-done.2, bf16[128,640]{1,0:T(8,128)(2,1)S(1)} %collective-permute-done.6.queries, bf16[128,640]{1,0:T(8,128)(2,1)S(1)} %collective-permute-done.1.kl, bf16[128,640]{1,0:T(8,128)(2,1)S(1)} %shard_map.83.rest_0_.km, ...), custom_call_target="tpu_custom_call" | custom-call | flops 125829120 | bytes 1331200 | tf_op jit(solution)/shard_map/pallas_call | solution.py:166
  52.1 6.9 %collective-permute-start.7 = (bf16[144,640]{1,0:T(8,128)(2,1)S(1)}, bf16[144,640]{1,0:T(8,128)(2,1)S(1)}, u32[]{:S(2)}, u32[]{:S(2)}) collective-permute-start(bf16[144,640]{1,0:T(8,128)(2,1)S(1)} %shard_map.87), channel_id=1, source_target_pairs={{0,496},{1,17},{2,498},{3,19},{16,0},{17,33},{18,2},{19,35},{32,16... | collective-permute-start | bytes 552968 | tf_op jit(solution)/shard_map/ppermute | solution.py:27
  59.0 0.0 copy-done.1
  59.0 0.0 copy-done.3
  59.0 1.5 %shard_map.85 = (f32[128,640]{1,0:T(8,128)S(1)}, f32[128,640]{1,0:T(8,128)S(1)}, f32[128,640]{1,0:T(8,128)S(1)}) custom-call(s32[3]{0:T(128)S(1)} %pad_add_fusion.place_ref, s32[17]{0:T(128)S(1)} %copy-done.2, s32[17]{0:T(128)S(1)} %copy-done.3, f32[50,640]{1,0:T(8,128)S(1)} %copy-done.1, bf16[128,640]{1,0:T(8,128)(2,1)S(1)} %shard_map.84.q, ...), custom_call_target="tpu_custom_call" | custom-call | flops 125829120 | bytes 2257920 | tf_op jit(solution)/shard_map/pallas_call | solution.py:166
  60.5 0.0 collective-permute-done.5.from_left
  60.5 1.5 %collective-permute-done.7.from_right = bf16[144,640]{1,0:T(8,128)(2,1)S(1)} collective-permute-done((bf16[144,640]{1,0:T(8,128)(2,1)S(1)}, bf16[144,640]{1,0:T(8,128)(2,1)S(1)}, u32[]{:S(2)}, u32[]{:S(2)}) %collective-permute-start.7) | collective-permute-done | bytes 184352 | tf_op jit(solution)/shard_map/ppermute | solution.py:27
  62.0 1.0 %shard_map.88 = bf16[128,640]{1,0:T(8,128)(2,1)} custom-call(f32[128,640]{1,0:T(8,128)S(1)} %get-tuple-element.8.gate, f32[128,640]{1,0:T(8,128)S(1)} %get-tuple-element.9.mixed, f32[128,640]{1,0:T(8,128)S(1)} %get-tuple-element.10.levels, bf16[144,640]{1,0:T(8,128)(2,1)S(1)} %collective-permute-done.5.from_left, ...), custom_call_target="tpu_custom_call" | custom-call | bytes 1515520 | tf_op jit(solution)/shard_map/pallas_call | solution.py:166
  (2 shorter events, 0.0 us)
Async XLA Ops:
  0.0 31.1 %collective-permute-start = (bf16[128,640]{1,0:T(8,128)(2,1)}, bf16[128,640]{1,0:T(8,128)(2,1)S(1)}, u32[]{:S(2)}, u32[]{:S(2)}) collective-permute-start(bf16[128,640]{1,0:T(8,128)(2,1)} %vm.5), channel_id=1, source_target_pairs={{0,48},{2,50},{16,64},{18,66},{32,80},{33,497},{34,82},{35,499},{4... | collective-permute-start | bytes 491528 | tf_op jit(solution)/shard_map/ppermute | solution.py:27
  7.6 5.8 %copy-start = (bf16[128,640]{1,0:T(8,128)(2,1)S(1)}, bf16[128,640]{1,0:T(8,128)(2,1)}, u32[]{:S(2)}) copy-start(bf16[128,640]{1,0:T(8,128)(2,1)} %vm.5) | copy-start | bytes 491524
  8.3 13.7 %copy-start.4 = (f32[640]{0:T(1024)S(1)}, f32[640]{0:T(1024)}, u32[]{:S(2)}) copy-start(f32[640]{0:T(1024)} %param.11) | copy-start | bytes 7684
  8.3 13.7 %all-to-all-start = ((f32[4,8,128]{2,1,0:T(8,128)}), f32[4,8,128]{2,1,0:T(8,128)S(1)}, u32[]{:S(2)}, u32[]{:S(2)}) async-start(f32[4,8,128]{2,1,0:T(8,128)} %shard_map.82), calls=%async_computation | async-start | bytes 32768 | tf_op jit(solution)/shard_map/all_to_all | solution.py:188
  13.4 8.7 %copy-start.5 = (f32[640]{0:T(1024)S(1)}, f32[640]{0:T(1024)}, u32[]{:S(2)}) copy-start(f32[640]{0:T(1024)} %param.12) | copy-start | bytes 7684
  13.4 27.1 %collective-permute-start.3 = (bf16[128,640]{1,0:T(8,128)(2,1)S(1)}, bf16[128,640]{1,0:T(8,128)(2,1)S(1)}, u32[]{:S(2)}, u32[]{:S(2)}) collective-permute-start(bf16[128,640]{1,0:T(8,128)(2,1)S(1)} %copy-done), channel_id=1, source_target_pairs={{1,49},{3,51},{17,65},{19,67},{32,496},{33,81},{34,498},{35,83},{4... | collective-permute-start | bytes 491528 | tf_op jit(solution)/shard_map/ppermute | solution.py:27
  22.2 18.3 %collective-permute-start.2 = (bf16[128,640]{1,0:T(8,128)(2,1)S(1)}, bf16[128,640]{1,0:T(8,128)(2,1)S(1)}, u32[]{:S(2)}, u32[]{:S(2)}) collective-permute-start(bf16[128,640]{1,0:T(8,128)(2,1)S(1)} %shard_map.83.rest_0_.km), channel_id=1, source_target_pairs={{1,49},{3,51},{17,65},{19,67},{32,496},{33,81},{34,498},{35,83},{4... | collective-permute-start | bytes 491528 | tf_op jit(solution)/shard_map/ppermute | solution.py:27
  29.2 17.6 %collective-permute-start.1 = (bf16[128,640]{1,0:T(8,128)(2,1)S(1)}, bf16[128,640]{1,0:T(8,128)(2,1)S(1)}, u32[]{:S(2)}, u32[]{:S(2)}) collective-permute-start(bf16[128,640]{1,0:T(8,128)(2,1)S(1)} %shard_map.83.rest_0_.km), channel_id=1, source_target_pairs={{0,48},{2,50},{16,64},{18,66},{32,80},{33,497},{34,82},{35,499},{4... | collective-permute-start | bytes 491528 | tf_op jit(solution)/shard_map/ppermute | solution.py:27
  31.2 15.6 %collective-permute-start.4 = (bf16[128,640]{1,0:T(8,128)(2,1)S(1)}, bf16[128,640]{1,0:T(8,128)(2,1)S(1)}, u32[]{:S(2)}, u32[]{:S(2)}) collective-permute-start(bf16[128,640]{1,0:T(8,128)(2,1)S(1)} %shard_map.84.q), channel_id=1, source_target_pairs={{0,496},{1,17},{2,498},{3,19},{16,0},{17,33},{18,2},{19,35},{32,16... | collective-permute-start | bytes 491528 | tf_op jit(solution)/shard_map/ppermute | solution.py:27
  38.5 12.3 %collective-permute-start.6 = (bf16[128,640]{1,0:T(8,128)(2,1)S(1)}, bf16[128,640]{1,0:T(8,128)(2,1)S(1)}, u32[]{:S(2)}, u32[]{:S(2)}) collective-permute-start(bf16[128,640]{1,0:T(8,128)(2,1)S(1)} %shard_map.84.q), channel_id=1, source_target_pairs={{0,16},{1,497},{2,18},{3,499},{16,32},{17,1},{18,34},{19,3},{32,48... | collective-permute-start | bytes 491528 | tf_op jit(solution)/shard_map/ppermute | solution.py:27
  40.4 6.4 %copy-start.2 = (s32[17]{0:T(128)S(1)}, s32[17]{0:T(128)}, u32[]{:S(2)}) copy-start(s32[17]{0:T(128)} %lengths_ref.5) | copy-start | bytes 208
  48.1 10.9 %copy-start.1 = (f32[50,640]{1,0:T(8,128)S(1)}, f32[50,640]{1,0:T(8,128)}, u32[]{:S(2)}) copy-start(f32[50,640]{1,0:T(8,128)} %table.1) | copy-start | bytes 384004
  48.1 10.9 %copy-start.3 = (s32[17]{0:T(128)S(1)}, s32[17]{0:T(128)}, u32[]{:S(2)}) copy-start(s32[17]{0:T(128)} %steps_ref.1) | copy-start | bytes 208
  48.1 12.4 %collective-permute-start.5 = (bf16[144,640]{1,0:T(8,128)(2,1)S(1)}, bf16[144,640]{1,0:T(8,128)(2,1)S(1)}, u32[]{:S(2)}, u32[]{:S(2)}) collective-permute-start(bf16[144,640]{1,0:T(8,128)(2,1)S(1)} %shard_map.86), channel_id=1, source_target_pairs={{0,16},{1,497},{2,18},{3,499},{16,32},{17,1},{18,34},{19,3},{32,48... | collective-permute-start | bytes 552968 | tf_op jit(solution)/shard_map/ppermute | solution.py:27
  52.1 9.9 %collective-permute-start.7 = (bf16[144,640]{1,0:T(8,128)(2,1)S(1)}, bf16[144,640]{1,0:T(8,128)(2,1)S(1)}, u32[]{:S(2)}, u32[]{:S(2)}) collective-permute-start(bf16[144,640]{1,0:T(8,128)(2,1)S(1)} %shard_map.87), channel_id=1, source_target_pairs={{0,496},{1,17},{2,498},{3,19},{16,0},{17,33},{18,2},{19,35},{32,16... | collective-permute-start | bytes 552968 | tf_op jit(solution)/shard_map/ppermute | solution.py:27

commit v4 on v3

--- a/solution.py
+++ b/solution.py
@@ -16,13 +16,13 @@
 EXTRA = 16
 
 
-def hop(value, steps):
+def hop(value, steps, by_core=False):
     count, parts = lax.axis_size("seq"), lax.axis_size("dp")
     pairs = []
     for source in range(count):
         for part in range(parts):
-            target = source + (steps if part % 2 == 0 else -steps)
-            if 0 <= target < count or (source, target % count) in ((2, count - 1), (count - FAR, 0)) or abs(steps) == 1:
+            target = source + (-steps if by_core and part % 2 else steps)
+            if 0 <= target < count or abs(steps) == 1 or (source, target % count) in ((2, count - 1), (count - FAR, 0)):
                 pairs.append((source * parts + part, target % count * parts + part))
     return lax.ppermute(value, ("seq", "dp"), pairs)
 
@@ -51,7 +51,7 @@
 
 
 def neighbour(place_ref, step):
-    block, count = place_ref[0] + step * place_ref[2], place_ref[1]
+    block, count = place_ref[0] + step, place_ref[1]
     return jnp.where(block < 0, block + count, jnp.where(block >= count, block - count, block))
 
 
@@ -83,32 +83,27 @@
     rest[-1][...] = (scaled * gain_ref[...]).astype(jnp.bfloat16)
 
 
-def attend(queries, keys, values, masks):
+def attend(queries, keys, values, mask):
     heads = range(queries.shape[1] // HD)
     at = [slice(head * HD, (head + 1) * HD) for head in heads]
     scores = [
-        [
-            jnp.where(
-                mask,
-                lax.dot_general(
-                    queries[:, at[h]], key[:, at[h]], (((1,), (1,)), ((), ())), preferred_element_type=jnp.float32
-                ),
-                LOW,
-            )
-            for key, mask in zip(keys, masks)
-        ]
+        lax.dot_general(
+            queries[:, at[h]],
+            jnp.concatenate([key[:, at[h]] for key in keys], axis=0),
+            (((1,), (1,)), ((), ())),
+            preferred_element_type=jnp.float32,
+        )
         for h in heads
     ]
-    highest = [jnp.max(functools.reduce(jnp.maximum, scores[h]), axis=1, keepdims=True) for h in heads]
-    weights = [[jnp.exp2((score - highest[h]) * SCALE2) for score in scores[h]] for h in heads]
-    total = [jnp.sum(functools.reduce(jnp.add, weights[h]), axis=1, keepdims=True) for h in heads]
+    scores = [jnp.where(mask, score, LOW) for score in scores]
+    highest = [jnp.max(score, axis=1, keepdims=True) for score in scores]
+    weights = [jnp.exp2((scores[h] - highest[h]) * SCALE2) for h in heads]
+    total = [jnp.sum(weight, axis=1, keepdims=True) for weight in weights]
     mixed = [
-        functools.reduce(
-            jnp.add,
-            [
-                jnp.dot(weight.astype(jnp.bfloat16), value[:, at[h]], preferred_element_type=jnp.float32)
-                for weight, value in zip(weights[h], values)
-            ],
+        jnp.dot(
+            weights[h].astype(jnp.bfloat16),
+            jnp.concatenate([value[:, at[h]] for value in values], axis=0),
+            preferred_element_type=jnp.float32,
         )
         for h in heads
     ]
@@ -118,8 +113,9 @@
 def guest_kernel(step, place_ref, lengths_ref, queries, kl, km, kr, vl, vm, vr, out):
     rows, width = queries.shape
     query_ids = row_clips(neighbour(place_ref, step), rows, lengths_ref)
-    masks = [query_ids == key_clips(neighbour(place_ref, far), rows, lengths_ref) for far in (-FAR, 0, FAR)]
-    for at, mixed, level in attend(queries, (kl, km, kr), (vl, vm, vr), masks):
+    key_ids = [key_clips(neighbour(place_ref, far * place_ref[2]), rows, lengths_ref) for far in (-FAR, 0, FAR)]
+    mask = query_ids == jnp.concatenate(key_ids, axis=1)
+    for at, mixed, level in attend(queries, (kl, km, kr), (vl, vm, vr), mask):
         out[:rows, at] = mixed.astype(jnp.bfloat16)
         rest = as_row(level)
         lines = []
@@ -134,8 +130,9 @@
 def home_kernel(place_ref, lengths_ref, steps_ref, table, q, kl, km, kr, vl, vm, vr, mixed_out, level_out, gate_out):
     rows, width = q.shape
     query_ids = row_clips(place_ref[0], rows, lengths_ref)
-    masks = [query_ids == key_clips(neighbour(place_ref, far), rows, lengths_ref) for far in (-FAR, 0, FAR)]
-    for at, mixed, level in attend(q, (kl, km, kr), (vl, vm, vr), masks):
+    key_ids = [key_clips(neighbour(place_ref, far * place_ref[2]), rows, lengths_ref) for far in (-FAR, 0, FAR)]
+    mask = query_ids == jnp.concatenate(key_ids, axis=1)
+    for at, mixed, level in attend(q, (kl, km, kr), (vl, vm, vr), mask):
         mixed_out[:, at] = mixed
         level_out[:, at] = jnp.broadcast_to(level, (rows, HD))
     gate = jnp.zeros((rows, width), jnp.float32)
@@ -182,7 +179,7 @@
     bf16 = functools.partial(jax.ShapeDtypeStruct, dtype=jnp.bfloat16)
     f32 = functools.partial(jax.ShapeDtypeStruct, dtype=jnp.float32)
 
-    v_near, v_next = hop(v_rows, FAR), hop(v_rows, -FAR)
+    v_near, v_next = hop(v_rows, FAR, True), hop(v_rows, -FAR, True)
     both = jnp.stack([q_rows, k_rows])
     (squares,) = call(squares_kernel, [f32((peers, 8, rows))], [], [both])
     squares = lax.all_to_all(squares, "head", 0, 0)
@@ -195,12 +192,12 @@
         [],
         [squares, both, q_gain.reshape(1, width), k_norm, v_near],
     )
-    k_near, k_next = hop(k_norm, FAR), hop(k_norm, -FAR)
-    q_near, q_next = hop(q_norm, 1), hop(q_norm, -1)
+    k_near, k_next = hop(k_norm, FAR, True), hop(k_norm, -FAR, True)
+    q_right, q_left = hop(q_norm, -1), hop(q_norm, 1)
     around = [k_near, k_norm, k_next, v_near, v_rows, v_next]
     flops = 4 * rows * 3 * rows * HD * heads_here
     returned = []
-    for queries, step in ((q_near, -1), (q_next, 1)):
+    for queries, step in ((q_right, 1), (q_left, -1)):
         (partial,) = call(
             functools.partial(guest_kernel, step),
             [bf16((rows + EXTRA, width))],
@@ -209,7 +206,7 @@
             flops,
         )
         returned.append(hop(partial, step))
-    from_right, from_left = returned
+    from_left, from_right = returned
     mixed, levels, gate = call(
         home_kernel,
         [f32((rows, width))] * 3,

time: 63.5 us -> 62 us (0.976)
  waiting for transfers between devices: 7.79 us -> 6.5 us
    ppermute x8, waiting for transfers between devices: 7.79 us -> 6.5 us  [hop(): return lax.ppermute(value, ('seq', 'dp'), pairs)]
where the time goes in v4:
time: 62 us; the launch traced here: 61.6 us
  starting transfers between devices  47.8 us (77%)
  waiting for transfers between devices  6.5 us (10%)
  Pallas kernels  5.9 us (10%)
  other arithmetic  1.11 us (2%)
    ppermute x8, starting transfers between devices, hop(): return lax.ppermute(value, ('seq', 'dp'), pairs)  42.8 us
    ppermute x8, waiting for transfers between devices, hop(): return lax.ppermute(value, ('seq', 'dp'), pairs)  6.5 us
    pallas_call x7, Pallas kernels, call(): pl.pallas_call(kernel, out_shape=outs, in_specs=space, out_specs=[pl.Bloc...  5.9 us
    all_to_all x1, starting transfers between devices, per_device(): squares = lax.all_to_all(squares, 'head', 0, 0)  5.04 us
  transfers between devices with their start and end apart: 9, of which 2 were waited for; matrix products, arithmetic and copies ran while one was open for 2% of the time, Pallas kernels for 8%

profile of v4, /device:TPU:14, one launch (start us, length us, event | category | flops | bytes accessed | tf_op | source)
XLA Modules:
  0.0 61.6 jit_solution(5010283566312684763)
XLA Ops:
  0.0 6.5 %collective-permute-start = (bf16[128,640]{1,0:T(8,128)(2,1)}, bf16[128,640]{1,0:T(8,128)(2,1)S(1)}, u32[]{:S(2)}, u32[]{:S(2)}) collective-permute-start(bf16[128,640]{1,0:T(8,128)(2,1)} %vm.5), channel_id=1, source_target_pairs={{0,48},{2,50},{16,64},{18,66},{32,80},{33,497},{34,82},{35,499},{4... | collective-permute-start | bytes 491528 | tf_op jit(solution)/shard_map/ppermute | solution.py:27
  6.5 1.0 %pad_maximum_fusion.both_ref = bf16[2,128,640]{2,1,0:T(8,128)(2,1)S(1)} fusion(bf16[1,128,640]{2,1,0:T(8,128)(2,1)} %bitcast.4, bf16[1,128,640]{2,1,0:T(8,128)(2,1)} %bitcast.5), kind=kLoop, calls=%fused_computation | loop fusion | flops 163840 | bytes 655360 | tf_op jit(solution)/shard_map/stack | solution.py:183
  7.6 0.0 copy-start
  7.6 0.8 %shard_map.82 = f32[4,8,128]{2,1,0:T(8,128)} custom-call(bf16[2,128,640]{2,1,0:T(8,128)(2,1)S(1)} %pad_maximum_fusion.both_ref), custom_call_target="tpu_custom_call" | custom-call | bytes 344064 | tf_op jit(solution)/shard_map/pallas_call | solution.py:163
  8.3 0.0 copy-start.4
  8.3 5.0 %all-to-all-start = ((f32[4,8,128]{2,1,0:T(8,128)}), f32[4,8,128]{2,1,0:T(8,128)S(1)}, u32[]{:S(2)}, u32[]{:S(2)}) async-start(f32[4,8,128]{2,1,0:T(8,128)} %shard_map.82), calls=%async_computation | async-start | bytes 32768 | tf_op jit(solution)/shard_map/all_to_all | solution.py:185
  13.4 0.0 copy-done
  13.4 0.0 copy-start.5
  13.4 8.6 %collective-permute-start.3 = (bf16[128,640]{1,0:T(8,128)(2,1)S(1)}, bf16[128,640]{1,0:T(8,128)(2,1)S(1)}, u32[]{:S(2)}, u32[]{:S(2)}) collective-permute-start(bf16[128,640]{1,0:T(8,128)(2,1)S(1)} %copy-done), channel_id=1, source_target_pairs={{1,49},{3,51},{17,65},{19,67},{32,496},{33,81},{34,498},{35,83},{4... | collective-permute-start | bytes 491528 | tf_op jit(solution)/shard_map/ppermute | solution.py:27
  22.0 0.0 copy-done.4
  22.1 0.0 copy-done.5
  22.1 0.0 all-to-all-done.squares_ref
  22.1 0.1 shard_map.83.rest_0_.km
  22.2 6.9 %collective-permute-start.2 = (bf16[128,640]{1,0:T(8,128)(2,1)S(1)}, bf16[128,640]{1,0:T(8,128)(2,1)S(1)}, u32[]{:S(2)}, u32[]{:S(2)}) collective-permute-start(bf16[128,640]{1,0:T(8,128)(2,1)S(1)} %shard_map.83.rest_0_.km), channel_id=1, source_target_pairs={{1,49},{3,51},{17,65},{19,67},{32,496},{33,81},{34,498},{35,83},{4... | collective-permute-start | bytes 491528 | tf_op jit(solution)/shard_map/ppermute | solution.py:27
  29.2 1.9 %collective-permute-start.1 = (bf16[128,640]{1,0:T(8,128)(2,1)S(1)}, bf16[128,640]{1,0:T(8,128)(2,1)S(1)}, u32[]{:S(2)}, u32[]{:S(2)}) collective-permute-start(bf16[128,640]{1,0:T(8,128)(2,1)S(1)} %shard_map.83.rest_0_.km), channel_id=1, source_target_pairs={{0,48},{2,50},{16,64},{18,66},{32,80},{33,497},{34,82},{35,499},{4... | collective-permute-start | bytes 491528 | tf_op jit(solution)/shard_map/ppermute | solution.py:27
  31.1 0.0 collective-permute-done.rest_1_.vl
  31.1 0.1 shard_map.84.q
  31.2 7.2 %collective-permute-start.4 = (bf16[128,640]{1,0:T(8,128)(2,1)S(1)}, bf16[128,640]{1,0:T(8,128)(2,1)S(1)}, u32[]{:S(2)}, u32[]{:S(2)}) collective-permute-start(bf16[128,640]{1,0:T(8,128)(2,1)S(1)} %shard_map.84.q), channel_id=1, source_target_pairs={{0,496},{1,497},{2,498},{3,499},{16,0},{17,1},{18,2},{19,3},{32,16... | collective-permute-start | bytes 491528 | tf_op jit(solution)/shard_map/ppermute | solution.py:27
  38.5 1.9 %collective-permute-start.6 = (bf16[128,640]{1,0:T(8,128)(2,1)S(1)}, bf16[128,640]{1,0:T(8,128)(2,1)S(1)}, u32[]{:S(2)}, u32[]{:S(2)}) collective-permute-start(bf16[128,640]{1,0:T(8,128)(2,1)S(1)} %shard_map.84.q), channel_id=1, source_target_pairs={{0,16},{1,17},{2,18},{3,19},{16,32},{17,33},{18,34},{19,35},{32,48... | collective-permute-start | bytes 491528 | tf_op jit(solution)/shard_map/ppermute | solution.py:27
  40.4 0.0 copy-start.2
  40.4 0.1 pad_add_fusion.place_ref
  40.5 0.0 collective-permute-done.3.vr
  40.5 0.0 collective-permute-done.2.kr
  40.5 4.5 %collective-permute-done.1.kl = bf16[128,640]{1,0:T(8,128)(2,1)S(1)} collective-permute-done((bf16[128,640]{1,0:T(8,128)(2,1)S(1)}, bf16[128,640]{1,0:T(8,128)(2,1)S(1)}, u32[]{:S(2)}, u32[]{:S(2)}) %collective-permute-start.1) | collective-permute-done | bytes 163872 | tf_op jit(solution)/shard_map/ppermute | solution.py:27
  45.0 0.0 collective-permute-done.4.queries
  45.0 0.0 copy-done.2
  45.0 1.2 %shard_map.86 = bf16[144,640]{1,0:T(8,128)(2,1)S(1)} custom-call(s32[3]{0:T(128)S(1)} %pad_add_fusion.place_ref, s32[17]{0:T(128)S(1)} %copy-done.2, bf16[128,640]{1,0:T(8,128)(2,1)S(1)} %collective-permute-done.4.queries, bf16[128,640]{1,0:T(8,128)(2,1)S(1)} %collective-permute-done.1.kl, bf16[128,640]{1,0:T(8,128)(2,1)S(1)} %shard_map.83.rest_0_.km, ...), custom_call_target="tpu_custom_call" | custom-call | flops 125829120 | bytes 1331200 | tf_op jit(solution)/shard_map/pallas_call | solution.py:163
  46.2 0.0 copy-start.1
  46.2 0.0 copy-start.3
  46.2 3.6 %collective-permute-start.5 = (bf16[144,640]{1,0:T(8,128)(2,1)S(1)}, bf16[144,640]{1,0:T(8,128)(2,1)S(1)}, u32[]{:S(2)}, u32[]{:S(2)}) collective-permute-start(bf16[144,640]{1,0:T(8,128)(2,1)S(1)} %shard_map.86), channel_id=1, source_target_pairs={{0,16},{1,17},{2,18},{3,19},{16,32},{17,33},{18,34},{19,35},{32,48... | collective-permute-start | bytes 552968 | tf_op jit(solution)/shard_map/ppermute | solution.py:27
  49.8 0.0 collective-permute-done.6.queries
  49.8 1.2 %shard_map.87 = bf16[144,640]{1,0:T(8,128)(2,1)S(1)} custom-call(s32[3]{0:T(128)S(1)} %pad_add_fusion.place_ref, s32[17]{0:T(128)S(1)} %copy-done.2, bf16[128,640]{1,0:T(8,128)(2,1)S(1)} %collective-permute-done.6.queries, bf16[128,640]{1,0:T(8,128)(2,1)S(1)} %collective-permute-done.1.kl, bf16[128,640]{1,0:T(8,128)(2,1)S(1)} %shard_map.83.rest_0_.km, ...), custom_call_target="tpu_custom_call" | custom-call | flops 125829120 | bytes 1331200 | tf_op jit(solution)/shard_map/pallas_call | solution.py:163
  51.0 6.0 %collective-permute-start.7 = (bf16[144,640]{1,0:T(8,128)(2,1)S(1)}, bf16[144,640]{1,0:T(8,128)(2,1)S(1)}, u32[]{:S(2)}, u32[]{:S(2)}) collective-permute-start(bf16[144,640]{1,0:T(8,128)(2,1)S(1)} %shard_map.87), channel_id=1, source_target_pairs={{0,496},{1,497},{2,498},{3,499},{16,0},{17,1},{18,2},{19,3},{32,16... | collective-permute-start | bytes 552968 | tf_op jit(solution)/shard_map/ppermute | solution.py:27
  57.0 0.0 copy-done.1
  57.0 0.0 copy-done.3
  57.0 1.5 %shard_map.85 = (f32[128,640]{1,0:T(8,128)S(1)}, f32[128,640]{1,0:T(8,128)S(1)}, f32[128,640]{1,0:T(8,128)S(1)}) custom-call(s32[3]{0:T(128)S(1)} %pad_add_fusion.place_ref, s32[17]{0:T(128)S(1)} %copy-done.2, s32[17]{0:T(128)S(1)} %copy-done.3, f32[50,640]{1,0:T(8,128)S(1)} %copy-done.1, bf16[128,640]{1,0:T(8,128)(2,1)S(1)} %shard_map.84.q, ...), custom_call_target="tpu_custom_call" | custom-call | flops 125829120 | bytes 2257920 | tf_op jit(solution)/shard_map/pallas_call | solution.py:163
  58.5 0.0 collective-permute-done.5.from_left
  58.5 2.0 %collective-permute-done.7.from_right = bf16[144,640]{1,0:T(8,128)(2,1)S(1)} collective-permute-done((bf16[144,640]{1,0:T(8,128)(2,1)S(1)}, bf16[144,640]{1,0:T(8,128)(2,1)S(1)}, u32[]{:S(2)}, u32[]{:S(2)}) %collective-permute-start.7) | collective-permute-done | bytes 184352 | tf_op jit(solution)/shard_map/ppermute | solution.py:27
  60.6 1.0 %shard_map.88 = bf16[128,640]{1,0:T(8,128)(2,1)} custom-call(f32[128,640]{1,0:T(8,128)S(1)} %get-tuple-element.8.gate, f32[128,640]{1,0:T(8,128)S(1)} %get-tuple-element.9.mixed, f32[128,640]{1,0:T(8,128)S(1)} %get-tuple-element.10.levels, bf16[144,640]{1,0:T(8,128)(2,1)S(1)} %collective-permute-done.5.from_left, ...), custom_call_target="tpu_custom_call" | custom-call | bytes 1515520 | tf_op jit(solution)/shard_map/pallas_call | solution.py:163
  (2 shorter events, 0.0 us)
Async XLA Ops:
  0.0 31.1 %collective-permute-start = (bf16[128,640]{1,0:T(8,128)(2,1)}, bf16[128,640]{1,0:T(8,128)(2,1)S(1)}, u32[]{:S(2)}, u32[]{:S(2)}) collective-permute-start(bf16[128,640]{1,0:T(8,128)(2,1)} %vm.5), channel_id=1, source_target_pairs={{0,48},{2,50},{16,64},{18,66},{32,80},{33,497},{34,82},{35,499},{4... | collective-permute-start | bytes 491528 | tf_op jit(solution)/shard_map/ppermute | solution.py:27
  7.6 5.8 %copy-start = (bf16[128,640]{1,0:T(8,128)(2,1)S(1)}, bf16[128,640]{1,0:T(8,128)(2,1)}, u32[]{:S(2)}) copy-start(bf16[128,640]{1,0:T(8,128)(2,1)} %vm.5) | copy-start | bytes 491524
  8.3 13.7 %copy-start.4 = (f32[640]{0:T(1024)S(1)}, f32[640]{0:T(1024)}, u32[]{:S(2)}) copy-start(f32[640]{0:T(1024)} %param.11) | copy-start | bytes 7684
  8.3 13.7 %all-to-all-start = ((f32[4,8,128]{2,1,0:T(8,128)}), f32[4,8,128]{2,1,0:T(8,128)S(1)}, u32[]{:S(2)}, u32[]{:S(2)}) async-start(f32[4,8,128]{2,1,0:T(8,128)} %shard_map.82), calls=%async_computation | async-start | bytes 32768 | tf_op jit(solution)/shard_map/all_to_all | solution.py:185
  13.4 8.7 %copy-start.5 = (f32[640]{0:T(1024)S(1)}, f32[640]{0:T(1024)}, u32[]{:S(2)}) copy-start(f32[640]{0:T(1024)} %param.12) | copy-start | bytes 7684
  13.4 27.1 %collective-permute-start.3 = (bf16[128,640]{1,0:T(8,128)(2,1)S(1)}, bf16[128,640]{1,0:T(8,128)(2,1)S(1)}, u32[]{:S(2)}, u32[]{:S(2)}) collective-permute-start(bf16[128,640]{1,0:T(8,128)(2,1)S(1)} %copy-done), channel_id=1, source_target_pairs={{1,49},{3,51},{17,65},{19,67},{32,496},{33,81},{34,498},{35,83},{4... | collective-permute-start | bytes 491528 | tf_op jit(solution)/shard_map/ppermute | solution.py:27
  22.2 18.3 %collective-permute-start.2 = (bf16[128,640]{1,0:T(8,128)(2,1)S(1)}, bf16[128,640]{1,0:T(8,128)(2,1)S(1)}, u32[]{:S(2)}, u32[]{:S(2)}) collective-permute-start(bf16[128,640]{1,0:T(8,128)(2,1)S(1)} %shard_map.83.rest_0_.km), channel_id=1, source_target_pairs={{1,49},{3,51},{17,65},{19,67},{32,496},{33,81},{34,498},{35,83},{4... | collective-permute-start | bytes 491528 | tf_op jit(solution)/shard_map/ppermute | solution.py:27
  29.2 15.8 %collective-permute-start.1 = (bf16[128,640]{1,0:T(8,128)(2,1)S(1)}, bf16[128,640]{1,0:T(8,128)(2,1)S(1)}, u32[]{:S(2)}, u32[]{:S(2)}) collective-permute-start(bf16[128,640]{1,0:T(8,128)(2,1)S(1)} %shard_map.83.rest_0_.km), channel_id=1, source_target_pairs={{0,48},{2,50},{16,64},{18,66},{32,80},{33,497},{34,82},{35,499},{4... | collective-permute-start | bytes 491528 | tf_op jit(solution)/shard_map/ppermute | solution.py:27
  31.2 13.7 %collective-permute-start.4 = (bf16[128,640]{1,0:T(8,128)(2,1)S(1)}, bf16[128,640]{1,0:T(8,128)(2,1)S(1)}, u32[]{:S(2)}, u32[]{:S(2)}) collective-permute-start(bf16[128,640]{1,0:T(8,128)(2,1)S(1)} %shard_map.84.q), channel_id=1, source_target_pairs={{0,496},{1,497},{2,498},{3,499},{16,0},{17,1},{18,2},{19,3},{32,16... | collective-permute-start | bytes 491528 | tf_op jit(solution)/shard_map/ppermute | solution.py:27
  38.5 11.3 %collective-permute-start.6 = (bf16[128,640]{1,0:T(8,128)(2,1)S(1)}, bf16[128,640]{1,0:T(8,128)(2,1)S(1)}, u32[]{:S(2)}, u32[]{:S(2)}) collective-permute-start(bf16[128,640]{1,0:T(8,128)(2,1)S(1)} %shard_map.84.q), channel_id=1, source_target_pairs={{0,16},{1,17},{2,18},{3,19},{16,32},{17,33},{18,34},{19,35},{32,48... | collective-permute-start | bytes 491528 | tf_op jit(solution)/shard_map/ppermute | solution.py:27
  40.4 4.6 %copy-start.2 = (s32[17]{0:T(128)S(1)}, s32[17]{0:T(128)}, u32[]{:S(2)}) copy-start(s32[17]{0:T(128)} %lengths_ref.5) | copy-start | bytes 208
  46.2 10.9 %copy-start.1 = (f32[50,640]{1,0:T(8,128)S(1)}, f32[50,640]{1,0:T(8,128)}, u32[]{:S(2)}) copy-start(f32[50,640]{1,0:T(8,128)} %table.1) | copy-start | bytes 384004
  46.2 10.9 %copy-start.3 = (s32[17]{0:T(128)S(1)}, s32[17]{0:T(128)}, u32[]{:S(2)}) copy-start(s32[17]{0:T(128)} %steps_ref.1) | copy-start | bytes 208
  46.2 12.3 %collective-permute-start.5 = (bf16[144,640]{1,0:T(8,128)(2,1)S(1)}, bf16[144,640]{1,0:T(8,128)(2,1)S(1)}, u32[]{:S(2)}, u32[]{:S(2)}) collective-permute-start(bf16[144,640]{1,0:T(8,128)(2,1)S(1)} %shard_map.86), channel_id=1, source_target_pairs={{0,16},{1,17},{2,18},{3,19},{16,32},{17,33},{18,34},{19,35},{32,48... | collective-permute-start | bytes 552968 | tf_op jit(solution)/shard_map/ppermute | solution.py:27
  51.0 9.6 %collective-permute-start.7 = (bf16[144,640]{1,0:T(8,128)(2,1)S(1)}, bf16[144,640]{1,0:T(8,128)(2,1)S(1)}, u32[]{:S(2)}, u32[]{:S(2)}) collective-permute-start(bf16[144,640]{1,0:T(8,128)(2,1)S(1)} %shard_map.87), channel_id=1, source_target_pairs={{0,496},{1,497},{2,498},{3,499},{16,0},{17,1},{18,2},{19,3},{32,16... | collective-permute-start | bytes 552968 | tf_op jit(solution)/shard_map/ppermute | solution.py:27

commit v5 on v4

--- a/solution.py
+++ b/solution.py
@@ -63,23 +63,29 @@
     return clip_of(block * rows + lax.broadcasted_iota(jnp.int32, (1, rows), 1), lengths_ref)
 
 
-def squares_kernel(both_ref, out_ref):
+def squares_kernel(q_ref, k_ref, out_ref, held, arrived):
+    copies = [
+        pltpu.make_async_copy(ref, held.at[index], arrived.at[index]) for index, ref in enumerate((q_ref, k_ref))
+    ]
+    for copy in copies:
+        copy.start()
     rows = out_ref.shape[2]
     lines = []
-    for index in range(2):
-        data = both_ref[index].astype(jnp.float32)
+    for index, copy in enumerate(copies):
+        copy.wait()
+        data = held[index].astype(jnp.float32)
         lines.append(as_row(jnp.sum(data * data, axis=1, keepdims=True)))
     lines = jnp.concatenate(lines + [jnp.zeros((6, rows), jnp.float32)], axis=0)
     for peer in range(out_ref.shape[0]):
         out_ref[peer] = lines
 
 
-def norm_kernel(index, squares_ref, both_ref, gain_ref, *rest):
+def norm_kernel(index, squares_ref, data_ref, gain_ref, *rest):
     total = squares_ref[0]
     for peer in range(1, squares_ref.shape[0]):
         total = total + squares_ref[peer]
     factors = lax.rsqrt(total / (HEADS * HD) + 1e-06)
-    scaled = both_ref[index].astype(jnp.float32) * as_column(factors[index : index + 1])
+    scaled = data_ref[...].astype(jnp.float32) * as_column(factors[index : index + 1])
     rest[-1][...] = (scaled * gain_ref[...]).astype(jnp.bfloat16)
 
 
@@ -180,17 +186,22 @@
     f32 = functools.partial(jax.ShapeDtypeStruct, dtype=jnp.float32)
 
     v_near, v_next = hop(v_rows, FAR, True), hop(v_rows, -FAR, True)
-    both = jnp.stack([q_rows, k_rows])
-    (squares,) = call(squares_kernel, [f32((peers, 8, rows))], [], [both])
+    squares = pl.pallas_call(
+        squares_kernel,
+        out_shape=f32((peers, 8, rows)),
+        in_specs=[pl.BlockSpec(memory_space=pl.ANY)] * 2,
+        out_specs=pl.BlockSpec(memory_space=pltpu.VMEM),
+        scratch_shapes=[pltpu.VMEM((2, rows, width), jnp.bfloat16), pltpu.SemaphoreType.DMA((2,))],
+    )(q_rows, k_rows)
     squares = lax.all_to_all(squares, "head", 0, 0)
     (k_norm,) = call(
-        functools.partial(norm_kernel, 1), [bf16((rows, width))], [], [squares, both, k_gain.reshape(1, width)]
+        functools.partial(norm_kernel, 1), [bf16((rows, width))], [], [squares, k_rows, k_gain.reshape(1, width)]
     )
     (q_norm,) = call(
         functools.partial(norm_kernel, 0),
         [bf16((rows, width))],
         [],
-        [squares, both, q_gain.reshape(1, width), k_norm, v_near],
+        [squares, q_rows, q_gain.reshape(1, width), k_norm, v_near],
     )
     k_near, k_next = hop(k_norm, FAR, True), hop(k_norm, -FAR, True)
     q_right, q_left = hop(q_norm, -1), hop(q_norm, 1)

time: 62 us -> 62 us (level)
  the two profiles are of different devices: /device:TPU:14 before, /device:TPU:22 now
where the time goes in v5:
time: 62 us; the launch traced here: 61.6 us
  starting transfers between devices  47.7 us (77%)
  Pallas kernels  6.91 us (11%)
  waiting for transfers between devices  6.63 us (11%)
    ppermute x8, starting transfers between devices, hop(): return lax.ppermute(value, ('seq', 'dp'), pairs)  42.9 us
    ppermute x8, waiting for transfers between devices, hop(): return lax.ppermute(value, ('seq', 'dp'), pairs)  6.62 us
    pallas_call x6, Pallas kernels, call(): pl.pallas_call(kernel, out_shape=outs, in_specs=space, out_specs=[pl.Bloc...  5.13 us
    all_to_all x1, starting transfers between devices, per_device(): squares = lax.all_to_all(squares, 'head', 0, 0)  4.81 us
    pallas_call x1, Pallas kernels, per_device(): pl.pallas_call(squares_kernel, out_shape=f32((peers, 8, rows)), in_specs=...  1.77 us
  transfers between devices with their start and end apart: 9, of which 3 were waited for; matrix products, arithmetic and copies ran while one was open for 0% of the time, Pallas kernels for 10%

profile of v5, /device:TPU:22, one launch (start us, length us, event | category | flops | bytes accessed | tf_op | source)
XLA Modules:
  0.0 61.6 jit_solution(12416823358312951059)
XLA Ops:
  0.0 0.0 copy-start
  0.0 0.0 copy-start.1
  0.0 6.7 %collective-permute-start = (bf16[128,640]{1,0:T(8,128)(2,1)}, bf16[128,640]{1,0:T(8,128)(2,1)S(1)}, u32[]{:S(2)}, u32[]{:S(2)}) collective-permute-start(bf16[128,640]{1,0:T(8,128)(2,1)} %vm.5), channel_id=1, source_target_pairs={{0,48},{2,50},{16,64},{18,66},{32,80},{33,497},{34,82},{35,499},{4... | collective-permute-start | bytes 491528 | tf_op jit(solution)/shard_map/ppermute | solution.py:27
  6.7 1.8 %shard_map.82 = f32[4,8,128]{2,1,0:T(8,128)} custom-call(bf16[128,640]{1,0:T(8,128)(2,1)} %data_ref.3, bf16[128,640]{1,0:T(8,128)(2,1)} %data_ref.2), custom_call_target="tpu_custom_call" | custom-call | tf_op jit(solution)/shard_map/pallas_call | solution.py:189
  8.4 0.0 copy-start.6
  8.5 4.8 %all-to-all-start = ((f32[4,8,128]{2,1,0:T(8,128)}), f32[4,8,128]{2,1,0:T(8,128)S(1)}, u32[]{:S(2)}, u32[]{:S(2)}) async-start(f32[4,8,128]{2,1,0:T(8,128)} %shard_map.82), calls=%async_computation | async-start | bytes 32768 | tf_op jit(solution)/shard_map/all_to_all | solution.py:196
  13.3 0.0 copy-done
  13.3 0.0 copy-start.7
  13.3 8.6 %collective-permute-start.3 = (bf16[128,640]{1,0:T(8,128)(2,1)S(1)}, bf16[128,640]{1,0:T(8,128)(2,1)S(1)}, u32[]{:S(2)}, u32[]{:S(2)}) collective-permute-start(bf16[128,640]{1,0:T(8,128)(2,1)S(1)} %copy-done), channel_id=1, source_target_pairs={{1,49},{3,51},{17,65},{19,67},{32,496},{33,81},{34,498},{35,83},{4... | collective-permute-start | bytes 491528 | tf_op jit(solution)/shard_map/ppermute | solution.py:27
  21.9 0.0 copy-done.6
  21.9 0.0 copy-done.7
  22.0 0.0 copy-start.2
  22.0 0.0 all-to-all-done.squares_ref
  22.0 0.0 copy-done.1
  22.0 0.1 shard_map.83.rest_0_.km
  22.1 6.9 %collective-permute-start.2 = (bf16[128,640]{1,0:T(8,128)(2,1)S(1)}, bf16[128,640]{1,0:T(8,128)(2,1)S(1)}, u32[]{:S(2)}, u32[]{:S(2)}) collective-permute-start(bf16[128,640]{1,0:T(8,128)(2,1)S(1)} %shard_map.83.rest_0_.km), channel_id=1, source_target_pairs={{1,49},{3,51},{17,65},{19,67},{32,496},{33,81},{34,498},{35,83},{4... | collective-permute-start | bytes 491528 | tf_op jit(solution)/shard_map/ppermute | solution.py:27
  29.1 1.9 %collective-permute-start.1 = (bf16[128,640]{1,0:T(8,128)(2,1)S(1)}, bf16[128,640]{1,0:T(8,128)(2,1)S(1)}, u32[]{:S(2)}, u32[]{:S(2)}) collective-permute-start(bf16[128,640]{1,0:T(8,128)(2,1)S(1)} %shard_map.83.rest_0_.km), channel_id=1, source_target_pairs={{0,48},{2,50},{16,64},{18,66},{32,80},{33,497},{34,82},{35,499},{4... | collective-permute-start | bytes 491528 | tf_op jit(solution)/shard_map/ppermute | solution.py:27
  31.0 0.0 collective-permute-done.rest_1_.vl
  31.0 0.0 copy-done.2
  31.0 0.1 shard_map.84.q
  31.2 7.2 %collective-permute-start.4 = (bf16[128,640]{1,0:T(8,128)(2,1)S(1)}, bf16[128,640]{1,0:T(8,128)(2,1)S(1)}, u32[]{:S(2)}, u32[]{:S(2)}) collective-permute-start(bf16[128,640]{1,0:T(8,128)(2,1)S(1)} %shard_map.84.q), channel_id=1, source_target_pairs={{0,496},{1,497},{2,498},{3,499},{16,0},{17,1},{18,2},{19,3},{32,16... | collective-permute-start | bytes 491528 | tf_op jit(solution)/shard_map/ppermute | solution.py:27
  38.4 1.9 %collective-permute-start.6 = (bf16[128,640]{1,0:T(8,128)(2,1)S(1)}, bf16[128,640]{1,0:T(8,128)(2,1)S(1)}, u32[]{:S(2)}, u32[]{:S(2)}) collective-permute-start(bf16[128,640]{1,0:T(8,128)(2,1)S(1)} %shard_map.84.q), channel_id=1, source_target_pairs={{0,16},{1,17},{2,18},{3,19},{16,32},{17,33},{18,34},{19,35},{32,48... | collective-permute-start | bytes 491528 | tf_op jit(solution)/shard_map/ppermute | solution.py:27
  40.3 0.0 copy-start.4
  40.3 0.1 pad_add_fusion.place_ref
  40.4 0.0 collective-permute-done.3.vr
  40.4 0.0 collective-permute-done.2.kr
  40.4 3.8 %collective-permute-done.1.kl = bf16[128,640]{1,0:T(8,128)(2,1)S(1)} collective-permute-done((bf16[128,640]{1,0:T(8,128)(2,1)S(1)}, bf16[128,640]{1,0:T(8,128)(2,1)S(1)}, u32[]{:S(2)}, u32[]{:S(2)}) %collective-permute-start.1) | collective-permute-done | bytes 163872 | tf_op jit(solution)/shard_map/ppermute | solution.py:27
  44.2 0.0 collective-permute-done.4.queries
  44.2 0.0 copy-done.4
  44.2 1.2 %shard_map.86 = bf16[144,640]{1,0:T(8,128)(2,1)S(1)} custom-call(s32[3]{0:T(128)S(1)} %pad_add_fusion.place_ref, s32[17]{0:T(128)S(1)} %copy-done.4, bf16[128,640]{1,0:T(8,128)(2,1)S(1)} %collective-permute-done.4.queries, bf16[128,640]{1,0:T(8,128)(2,1)S(1)} %collective-permute-done.1.kl, bf16[128,640]{1,0:T(8,128)(2,1)S(1)} %shard_map.83.rest_0_.km, ...), custom_call_target="tpu_custom_call" | custom-call | flops 125829120 | bytes 1331200 | tf_op jit(solution)/shard_map/pallas_call | solution.py:169
  45.4 0.0 copy-start.3
  45.4 0.0 copy-start.5
  45.4 5.0 %collective-permute-start.5 = (bf16[144,640]{1,0:T(8,128)(2,1)S(1)}, bf16[144,640]{1,0:T(8,128)(2,1)S(1)}, u32[]{:S(2)}, u32[]{:S(2)}) collective-permute-start(bf16[144,640]{1,0:T(8,128)(2,1)S(1)} %shard_map.86), channel_id=1, source_target_pairs={{0,16},{1,17},{2,18},{3,19},{16,32},{17,33},{18,34},{19,35},{32,48... | collective-permute-start | bytes 552968 | tf_op jit(solution)/shard_map/ppermute | solution.py:27
  50.5 0.0 collective-permute-done.6.queries
  50.5 1.2 %shard_map.87 = bf16[144,640]{1,0:T(8,128)(2,1)S(1)} custom-call(s32[3]{0:T(128)S(1)} %pad_add_fusion.place_ref, s32[17]{0:T(128)S(1)} %copy-done.4, bf16[128,640]{1,0:T(8,128)(2,1)S(1)} %collective-permute-done.6.queries, bf16[128,640]{1,0:T(8,128)(2,1)S(1)} %collective-permute-done.1.kl, bf16[128,640]{1,0:T(8,128)(2,1)S(1)} %shard_map.83.rest_0_.km, ...), custom_call_target="tpu_custom_call" | custom-call | flops 125829120 | bytes 1331200 | tf_op jit(solution)/shard_map/pallas_call | solution.py:169
  51.7 4.6 %collective-permute-start.7 = (bf16[144,640]{1,0:T(8,128)(2,1)S(1)}, bf16[144,640]{1,0:T(8,128)(2,1)S(1)}, u32[]{:S(2)}, u32[]{:S(2)}) collective-permute-start(bf16[144,640]{1,0:T(8,128)(2,1)S(1)} %shard_map.87), channel_id=1, source_target_pairs={{0,496},{1,497},{2,498},{3,499},{16,0},{17,1},{18,2},{19,3},{32,16... | collective-permute-start | bytes 552968 | tf_op jit(solution)/shard_map/ppermute | solution.py:27
  56.3 0.0 copy-done.3
  56.3 0.0 copy-done.5
  56.3 1.5 %shard_map.85 = (f32[128,640]{1,0:T(8,128)S(1)}, f32[128,640]{1,0:T(8,128)S(1)}, f32[128,640]{1,0:T(8,128)S(1)}) custom-call(s32[3]{0:T(128)S(1)} %pad_add_fusion.place_ref, s32[17]{0:T(128)S(1)} %copy-done.4, s32[17]{0:T(128)S(1)} %copy-done.5, f32[50,640]{1,0:T(8,128)S(1)} %copy-done.3, bf16[128,640]{1,0:T(8,128)(2,1)S(1)} %shard_map.84.q, ...), custom_call_target="tpu_custom_call" | custom-call | flops 125829120 | bytes 2257920 | tf_op jit(solution)/shard_map/pallas_call | solution.py:169
  57.7 0.4 collective-permute-done.5.from_left
  58.2 2.4 %collective-permute-done.7.from_right = bf16[144,640]{1,0:T(8,128)(2,1)S(1)} collective-permute-done((bf16[144,640]{1,0:T(8,128)(2,1)S(1)}, bf16[144,640]{1,0:T(8,128)(2,1)S(1)}, u32[]{:S(2)}, u32[]{:S(2)}) %collective-permute-start.7) | collective-permute-done | bytes 184352 | tf_op jit(solution)/shard_map/ppermute | solution.py:27
  60.6 1.0 %shard_map.88 = bf16[128,640]{1,0:T(8,128)(2,1)} custom-call(f32[128,640]{1,0:T(8,128)S(1)} %get-tuple-element.8.gate, f32[128,640]{1,0:T(8,128)S(1)} %get-tuple-element.9.mixed, f32[128,640]{1,0:T(8,128)S(1)} %get-tuple-element.10.levels, bf16[144,640]{1,0:T(8,128)(2,1)S(1)} %collective-permute-done.5.from_left, ...), custom_call_target="tpu_custom_call" | custom-call | bytes 1515520 | tf_op jit(solution)/shard_map/pallas_call | solution.py:169
  (2 shorter events, 0.0 us)
Async XLA Ops:
  0.0 13.3 %copy-start = (bf16[128,640]{1,0:T(8,128)(2,1)S(1)}, bf16[128,640]{1,0:T(8,128)(2,1)}, u32[]{:S(2)}) copy-start(bf16[128,640]{1,0:T(8,128)(2,1)} %vm.5) | copy-start | bytes 491524
  0.0 22.0 %copy-start.1 = (bf16[128,640]{1,0:T(8,128)(2,1)S(1)}, bf16[128,640]{1,0:T(8,128)(2,1)}, u32[]{:S(2)}) copy-start(bf16[128,640]{1,0:T(8,128)(2,1)} %data_ref.2) | copy-start | bytes 491524
  0.0 31.0 %collective-permute-start = (bf16[128,640]{1,0:T(8,128)(2,1)}, bf16[128,640]{1,0:T(8,128)(2,1)S(1)}, u32[]{:S(2)}, u32[]{:S(2)}) collective-permute-start(bf16[128,640]{1,0:T(8,128)(2,1)} %vm.5), channel_id=1, source_target_pairs={{0,48},{2,50},{16,64},{18,66},{32,80},{33,497},{34,82},{35,499},{4... | collective-permute-start | bytes 491528 | tf_op jit(solution)/shard_map/ppermute | solution.py:27
  8.4 13.5 %copy-start.6 = (f32[640]{0:T(1024)S(1)}, f32[640]{0:T(1024)}, u32[]{:S(2)}) copy-start(f32[640]{0:T(1024)} %param.11) | copy-start | bytes 7684
  8.5 13.5 %all-to-all-start = ((f32[4,8,128]{2,1,0:T(8,128)}), f32[4,8,128]{2,1,0:T(8,128)S(1)}, u32[]{:S(2)}, u32[]{:S(2)}) async-start(f32[4,8,128]{2,1,0:T(8,128)} %shard_map.82), calls=%async_computation | async-start | bytes 32768 | tf_op jit(solution)/shard_map/all_to_all | solution.py:196
  13.3 8.7 %copy-start.7 = (f32[640]{0:T(1024)S(1)}, f32[640]{0:T(1024)}, u32[]{:S(2)}) copy-start(f32[640]{0:T(1024)} %param.12) | copy-start | bytes 7684
  13.3 27.2 %collective-permute-start.3 = (bf16[128,640]{1,0:T(8,128)(2,1)S(1)}, bf16[128,640]{1,0:T(8,128)(2,1)S(1)}, u32[]{:S(2)}, u32[]{:S(2)}) collective-permute-start(bf16[128,640]{1,0:T(8,128)(2,1)S(1)} %copy-done), channel_id=1, source_target_pairs={{1,49},{3,51},{17,65},{19,67},{32,496},{33,81},{34,498},{35,83},{4... | collective-permute-start | bytes 491528 | tf_op jit(solution)/shard_map/ppermute | solution.py:27
  22.0 9.0 %copy-start.2 = (bf16[128,640]{1,0:T(8,128)(2,1)S(1)}, bf16[128,640]{1,0:T(8,128)(2,1)}, u32[]{:S(2)}) copy-start(bf16[128,640]{1,0:T(8,128)(2,1)} %data_ref.3) | copy-start | bytes 491524
  22.1 18.3 %collective-permute-start.2 = (bf16[128,640]{1,0:T(8,128)(2,1)S(1)}, bf16[128,640]{1,0:T(8,128)(2,1)S(1)}, u32[]{:S(2)}, u32[]{:S(2)}) collective-permute-start(bf16[128,640]{1,0:T(8,128)(2,1)S(1)} %shard_map.83.rest_0_.km), channel_id=1, source_target_pairs={{1,49},{3,51},{17,65},{19,67},{32,496},{33,81},{34,498},{35,83},{4... | collective-permute-start | bytes 491528 | tf_op jit(solution)/shard_map/ppermute | solution.py:27
  29.1 15.1 %collective-permute-start.1 = (bf16[128,640]{1,0:T(8,128)(2,1)S(1)}, bf16[128,640]{1,0:T(8,128)(2,1)S(1)}, u32[]{:S(2)}, u32[]{:S(2)}) collective-permute-start(bf16[128,640]{1,0:T(8,128)(2,1)S(1)} %shard_map.83.rest_0_.km), channel_id=1, source_target_pairs={{0,48},{2,50},{16,64},{18,66},{32,80},{33,497},{34,82},{35,499},{4... | collective-permute-start | bytes 491528 | tf_op jit(solution)/shard_map/ppermute | solution.py:27
  31.2 13.0 %collective-permute-start.4 = (bf16[128,640]{1,0:T(8,128)(2,1)S(1)}, bf16[128,640]{1,0:T(8,128)(2,1)S(1)}, u32[]{:S(2)}, u32[]{:S(2)}) collective-permute-start(bf16[128,640]{1,0:T(8,128)(2,1)S(1)} %shard_map.84.q), channel_id=1, source_target_pairs={{0,496},{1,497},{2,498},{3,499},{16,0},{17,1},{18,2},{19,3},{32,16... | collective-permute-start | bytes 491528 | tf_op jit(solution)/shard_map/ppermute | solution.py:27
  38.4 12.1 %collective-permute-start.6 = (bf16[128,640]{1,0:T(8,128)(2,1)S(1)}, bf16[128,640]{1,0:T(8,128)(2,1)S(1)}, u32[]{:S(2)}, u32[]{:S(2)}) collective-permute-start(bf16[128,640]{1,0:T(8,128)(2,1)S(1)} %shard_map.84.q), channel_id=1, source_target_pairs={{0,16},{1,17},{2,18},{3,19},{16,32},{17,33},{18,34},{19,35},{32,48... | collective-permute-start | bytes 491528 | tf_op jit(solution)/shard_map/ppermute | solution.py:27
  40.3 3.9 %copy-start.4 = (s32[17]{0:T(128)S(1)}, s32[17]{0:T(128)}, u32[]{:S(2)}) copy-start(s32[17]{0:T(128)} %lengths_ref.5) | copy-start | bytes 208
  45.4 10.9 %copy-start.3 = (f32[50,640]{1,0:T(8,128)S(1)}, f32[50,640]{1,0:T(8,128)}, u32[]{:S(2)}) copy-start(f32[50,640]{1,0:T(8,128)} %table.1) | copy-start | bytes 384004
  45.4 10.8 %copy-start.5 = (s32[17]{0:T(128)S(1)}, s32[17]{0:T(128)}, u32[]{:S(2)}) copy-start(s32[17]{0:T(128)} %steps_ref.1) | copy-start | bytes 208
  45.4 12.7 %collective-permute-start.5 = (bf16[144,640]{1,0:T(8,128)(2,1)S(1)}, bf16[144,640]{1,0:T(8,128)(2,1)S(1)}, u32[]{:S(2)}, u32[]{:S(2)}) collective-permute-start(bf16[144,640]{1,0:T(8,128)(2,1)S(1)} %shard_map.86), channel_id=1, source_target_pairs={{0,16},{1,17},{2,18},{3,19},{16,32},{17,33},{18,34},{19,35},{32,48... | collective-permute-start | bytes 552968 | tf_op jit(solution)/shard_map/ppermute | solution.py:27
  51.7 8.9 %collective-permute-start.7 = (bf16[144,640]{1,0:T(8,128)(2,1)S(1)}, bf16[144,640]{1,0:T(8,128)(2,1)S(1)}, u32[]{:S(2)}, u32[]{:S(2)}) collective-permute-start(bf16[144,640]{1,0:T(8,128)(2,1)S(1)} %shard_map.87), channel_id=1, source_target_pairs={{0,496},{1,497},{2,498},{3,499},{16,0},{17,1},{18,2},{19,3},{32,16... | collective-permute-start | bytes 552968 | tf_op jit(solution)/shard_map/ppermute | solution.py:27
